TPU v7x, 512 devices: a whole 4x4x16 slice. The times are simulated.
512 devices in a mesh: row: 32 (over z, core), col: 16 (over y, x).
Axes of the slice: x: 4, y: 4, z: 16, core: 2. Of those that a mesh axis runs over, the one named last changes fastest.
Arguments:
- a_blocks: bfloat16 [32, 16, 16, 320, 320], P('row', 'col'), may hold values from -0.3125 to 0.3125
- slot_row: int32 [32, 16, 16], P('row', 'col'), may hold values from 0 to 3
- slot_col: int32 [32, 16, 16], P('row', 'col'), may hold values from 0 to 7
- slot_count: int32 [32, 16], P('row', 'col'), may hold values from 1 to 16, as said below
- p_blocks: bfloat16 [128, 320, 64], P('row'), may hold values from -1.5 to 1.5
- aggregate: int32 [128], P('row'), may hold values from 0 to 31
- relayout: int32 [32], replicated, may hold values from 0 to 31, as said below
Outputs:
- coarse_relaid: float32 [32, 64, 2048], P('row')
Inputs may be any that keep to these rules, and one draw needn't show every extreme that they name: `slot_count`: each list holds 1 to 16 live blocks, and some list holds 16 in every draw. relayout is a permutation of the 32 coarse block rows.
All inputs are finite; a program needn't handle non-finite values.
Results may differ from a plain program's by a relative error of at most 0.0003.
Values may be sent and summed in bfloat16 or wider, within the bound.
A program may use at most 64 MiB of HBM per device.

v0:
```python
import jax
import jax.numpy as jnp
from jax import lax
from jax.sharding import PartitionSpec as P


def on_device(a_blocks, slot_row, slot_col, slot_count, p_blocks, aggregate, relayout):
    highest = lax.Precision.HIGHEST
    row_devices = lax.axis_size("row")
    col_devices = lax.axis_size("col")
    fine_rows = p_blocks.shape[0]
    slot_total = a_blocks.shape[2]
    col_blocks = fine_rows * row_devices // col_devices
    coarse = relayout.shape[0]
    width = p_blocks.shape[2]
    col_index = lax.axis_index("col")
    all_p, all_agg = (
        lax.all_gather(p_blocks, "row", axis=0, tiled=True),
        lax.all_gather(aggregate, "row", axis=0, tiled=True),
    )
    col_p = lax.dynamic_slice_in_dim(all_p, col_index * col_blocks, col_blocks, 0)
    col_agg = lax.dynamic_slice_in_dim(all_agg, col_index * col_blocks, col_blocks, 0)
    blocks = a_blocks[0, 0]
    slot_rows = slot_row[0, 0]
    slot_cols = slot_col[0, 0]
    live_count = slot_count[0, 0]
    picked = jnp.take(col_p, slot_cols, axis=0)
    products = jnp.einsum("sab,sbk->sak", blocks, picked, preferred_element_type=jnp.float32)
    live_slot = jnp.arange(slot_total, dtype=jnp.int32) < live_count
    row_onehot = (
        (slot_rows[None, :] == jnp.arange(fine_rows, dtype=jnp.int32)[:, None]) & live_slot[None, :]
    ).astype(jnp.float32)
    col_labels = jnp.take(col_agg, slot_cols)
    col_onehot = (col_labels[:, None] == jnp.arange(coarse, dtype=jnp.int32)[None, :]).astype(
        jnp.float32
    )
    weights = row_onehot[:, :, None] * col_onehot[None]
    applied = jnp.einsum("isq,sak->iaqk", weights, products, precision=highest)
    projected = jnp.einsum(
        "iam,iaqk->iqmk", p_blocks.astype(jnp.float32), applied, precision=highest
    )
    shared = lax.psum_scatter(projected, "col", scatter_dimension=1, tiled=True)
    target = jnp.arange(coarse, dtype=jnp.int32)
    agg_onehot = (aggregate[None, :] == target[:, None]).astype(jnp.float32)
    stacked = jnp.einsum("pi,iqmk->pqmk", agg_onehot, shared, precision=highest)
    owned = lax.psum_scatter(stacked, "row", scatter_dimension=0, tiled=True)
    gathered = lax.all_gather(owned, "row", axis=0, tiled=True)
    first_row = lax.axis_index("row") * owned.shape[0]
    wanted = lax.dynamic_slice_in_dim(relayout, first_row, owned.shape[0], 0)
    owned = jnp.take(gathered, wanted, axis=0)
    flattened = owned.transpose(0, 2, 1, 3).reshape(owned.shape[0], width, owned.shape[1] * width)
    return lax.all_gather(flattened, "col", axis=2, tiled=True)


def solution(mesh):
    return jax.shard_map(
        on_device,
        mesh=mesh,
        in_specs=(
            P("row", "col", None, None, None),
            P("row", "col", None),
            P("row", "col", None),
            P("row", "col"),
            P("row", None, None),
            P("row"),
            P(),
        ),
        out_specs=P("row", None, None),
        check_vma=False,
    )
```

profile of v0, /device:TPU:1, one launch (start us, length us, event | category | flops | bytes accessed | tf_op | source)
XLA Modules:
  0.0 424.7 jit_solution(18237705022358265350)
XLA Ops:
  6.5 0.0 all-gather.3.cloned.1.call-start
  6.5 0.7 all-gather.3.cloned.1.call-update
  7.3 0.0 reduce-scatter.3.cloned.1.call-start
  8.0 1.3 dynamic-slice.4
  9.9 0.9 dynamic-update-slice.1
  10.7 24.4 %all-reduce = s32[128]{0:T(128)S(1)} all-reduce(s32[128]{0:T(128)S(1)} %dynamic-update-slice.1), channel_id=1, replica_groups=mesh['row'=32,'col'=16] {'row'}, use_global_device_ids=true, to_apply=%add | all-reduce | flops 128 | bytes 1024
  35.2 0.1 dynamic_slice.11
  35.3 0.7 fusion.28
  35.9 0.7 gather_fusion.1
  36.6 0.7 broadcast_select_fusion
  37.3 0.7 fusion.26
  37.9 0.1 fusion.22
  38.0 54.1 %all-gather.3.cloned.1.call-done = bf16[128,320,64]{1,2,0:T(8,128)(2,1)} async-done(((bf16[4,320,64]{1,2,0:T(8,128)(2,1)}), bf16[128,320,64]{1,2,0:T(8,128)(2,1)}) %all-gather.3.cloned.1.call-update) | async-done | bytes 5242896 | tf_op jit(solution)/shard_map/all_gather | solution.py:18
  92.1 1.0 constant_dynamic-slice_fusion
  93.1 0.7 gather_fusion
  93.8 3.4 fusion.8
  97.3 0.0 copy-start
  97.3 10.2 %convolution_bitcast_fusion = f32[4,320,32,64]{1,2,0,3:T(8,128)S(1)} fusion(f32[16,320,64,1]{1,2,0,3:T(8,128)S(1)} %fusion.8, f32[16,32]{1,0:T(8,128)S(1)} %fusion.22, f32[4,16]{1,0:T(4,128)S(1)} %fusion.26), kind=kOutput, calls=%fused_computation.4 | convolution fusion | flops 503318528 | bytes 11798784 | tf_op jit(solution)/shard_map/isq,sak->iaqk/dot_general | solution.py:38
  107.5 0.0 copy-done
  107.5 7.7 %fusion.4 = f32[4,32,64,64]{2,1,3,0:T(8,128)} fusion(f32[4,320,32,64]{1,2,0,3:T(8,128)S(1)} %convolution_bitcast_fusion, bf16[4,320,64]{1,2,0:T(8,128)(2,1)S(1)} %copy-done), kind=kOutput, calls=%fused_computation.7 | convolution fusion | flops 2013265920 | bytes 12746752 | tf_op jit(solution)/shard_map/iam,iaqk->iqmk/dot_general | solution.py:39
  115.2 5.3 %copy.11 = f32[4,32,64,64]{3,2,0,1:T(8,128)} copy(f32[4,32,64,64]{2,1,3,0:T(8,128)} %fusion.4) | data formatting | bytes 4194304 | tf_op jit(solution)/shard_map/iam,iaqk->iqmk/transpose | solution.py:39
  120.5 0.0 copy-start.1
  120.5 0.0 reduce-scatter.3.cloned.1.call-update
  120.5 0.0 copy-start.2
  120.5 0.0 reduce-scatter.5.cloned.1.call-start
  120.5 88.3 %reduce-scatter.3.cloned.1.call-done = f32[4,2,64,64]{3,2,0,1:T(8,128)} async-done(((f32[4,32,64,64]{3,2,0,1:T(8,128)}), f32[4,2,64,64]{3,2,0,1:T(8,128)}) %reduce-scatter.3.cloned.1.call-update) | async-done | bytes 131088 | tf_op jit(solution)/shard_map/reduce_scatter | solution.py:42
  208.8 0.0 copy-done.1
  208.8 2.1 fusion.14
  210.9 2.6 copy.13
  213.4 0.0 reduce-scatter.5.cloned.1.call-update
  213.5 0.0 all-gather.5.cloned.1.call-start
  213.5 107.9 %reduce-scatter.5.cloned.1.call-done = f32[1,2,64,64]{3,2,1,0:T(8,128)} async-done(((f32[32,2,64,64]{3,2,1,0:T(8,128)}), f32[1,2,64,64]{3,2,1,0:T(8,128)}) %reduce-scatter.5.cloned.1.call-update) | async-done | bytes 32784 | tf_op jit(solution)/shard_map/reduce_scatter | solution.py:46
  321.4 0.0 all-gather.5.cloned.1.call-update
  321.5 0.0 copy-done.2
  321.5 0.6 dynamic_slice.9
  324.0 72.5 %all-gather.5.cloned.1.call-done = f32[32,2,64,64]{3,2,1,0:T(8,128)} async-done(((f32[1,2,64,64]{3,2,1,0:T(8,128)}), f32[32,2,64,64]{3,2,1,0:T(8,128)}) %all-gather.5.cloned.1.call-update) | async-done | bytes 1048592 | tf_op jit(solution)/shard_map/all_gather | solution.py:47
  396.5 0.8 fusion.17
  397.3 0.1 copy.14
  397.4 0.1 reshape.121
  397.5 19.8 %all_gather.15 = f32[1,64,2048]{2,1,0:T(8,128)S(1)} all-gather(f32[1,64,128]{2,1,0:T(8,128)S(1)} %reshape.121), channel_id=1, replica_groups=mesh['row'=32,'col'=16] {'col'}, dimensions={2}, use_global_device_ids=true | all-gather | bytes 557056 | tf_op jit(solution)/shard_map/all_gather | solution.py:52
  417.3 0.8 copy.35
  (3 shorter events, 0.0 us)
Async XLA Ops:
  6.5 85.5 %all-gather.3.cloned.1.call-start = ((), (), s32[]{:S(2)}) async-start(), calls=%async_computation.2 | async-start | bytes 6488064 | tf_op jit(solution)/shard_map/all_gather | solution.py:18
  7.3 201.5 %reduce-scatter.3.cloned.1.call-start = ((), (), s32[]{:S(2)}) async-start(), calls=%async_computation.3 | async-start | bytes 4456448 | tf_op jit(solution)/shard_map/reduce_scatter | solution.py:42
  97.3 10.2 %copy-start = (bf16[4,320,64]{1,2,0:T(8,128)(2,1)S(1)}, bf16[4,320,64]{1,2,0:T(8,128)(2,1)}, u32[]{:S(2)}) copy-start(bf16[4,320,64]{1,2,0:T(8,128)(2,1)} %param.11) | copy-start | bytes 491524
  120.5 88.3 %copy-start.1 = (s32[4]{0:T(128)S(1)}, s32[4]{0:T(128)}, u32[]{:S(2)}) copy-start(s32[4]{0:T(128)} %param.12) | copy-start | bytes 52
  120.5 201.0 %copy-start.2 = (s32[32]{0:T(128)S(1)}, s32[32]{0:T(128)}, u32[]{:S(2)}) copy-start(s32[32]{0:T(128)} %param.13) | copy-start | bytes 388
  120.5 201.0 %reduce-scatter.5.cloned.1.call-start = ((), (), s32[]{:S(2)}) async-start(), calls=%async_computation.4 | async-start | bytes 2162688 | tf_op jit(solution)/shard_map/reduce_scatter | solution.py:46
  213.5 183.0 %all-gather.5.cloned.1.call-start = ((), (), s32[]{:S(2)}) async-start(), calls=%async_computation.5 | async-start | bytes 2162688 | tf_op jit(solution)/shard_map/all_gather | solution.py:47
Sparse Core Ops, SparseCore 0:
  9.5 82.5 all-gather.2
  120.6 88.1 reduce-scatter.2
  213.6 107.8 reduce-scatter.4
  323.4 73.0 all-gather.4
where the time goes:
time: 429 us; the launch traced here: 425 us
  waiting for transfers between devices  324 us (76%)
  blocking collectives  44.3 us (10%)
  matrix products  23.4 us (5%)
  between operations  16.5 us (4%)
  local copies, waits for them, and re-layouts  14 us (3%)
    reduce_scatter x1, waiting for transfers between devices, on_device(): owned = lax.psum_scatter(stacked, 'row', scatter_dimension=0, tiled=True)  108 us
    reduce_scatter x1, waiting for transfers between devices, on_device(): shared = lax.psum_scatter(projected, 'col', scatter_dimension=1, tiled=True)  88.3 us
    all_gather x1, waiting for transfers between devices, on_device(): gathered = lax.all_gather(owned, 'row', axis=0, tiled=True)  72.5 us
    all_gather x1, waiting for transfers between devices, on_device(): lax.all_gather(p_blocks, 'row', axis=0, tiled=True)  54.1 us
    unnamed x1, blocking collectives  24.4 us
    all_gather x1, blocking collectives, on_device(): return lax.all_gather(flattened, 'col', axis=2, tiled=True)  19.8 us
    dot_general x1, matrix products, on_device(): applied = jnp.einsum('isq,sak->iaqk', weights, products, precision=highest)  10.2 us
  transfers between devices with their start and end apart: 4, of which 4 were waited for; matrix products, arithmetic and copies ran while one was open for 1% of the time, Pallas kernels for 0%

commit v1 on v0

v1 whole, which is shorter than its diff:
```python
import functools

import jax
import jax.numpy as jnp
from jax import lax
from jax.experimental import pallas as pl
from jax.experimental.pallas import tpu as pltpu
from jax.sharding import PartitionSpec as P

MESH = pl.DeviceIdType.MESH

NX, NY, NZ = 4, 4, 16
TREE = (8, 5, 11, 2, 14)
FAR = (2, 14, 4, 12, 6, 10, 8)
RING = (1, 15, 2, 14, 4, 12, 5, 11, 6, 10, 8)
F32 = jnp.float32
BF16 = jnp.bfloat16


def kernel(
    a_ref, rows_ref, cols_ref, count_ref, p_ref, agg_ref, relay_ref, out_ref,
    a_buf, pt, lhl, p_buf, agg_mine, agg_col, agg_quad, last_vec, col_s, quad_s, last_s, key_s,
    run, d_a, d_b, r_a, r_b, e_a, e_b, r2_a, r2_b, quad, run_z, ob, rz, tile, gat,
    loc_sem, sm_sem, p_ssem, p_rsem, f_ssem, sib_ssem, sib_rsem, ag_ssem, ag_rsem, af_ssem, as_ssem, as_rsem,
    q_ssem, q_rsem, x_ssem, x_rsem, x2_ssem, x2_rsem, z_ssem, z_rsem, w_ssem, w_rsem, o_ssem, o_rsem,
):
    row = lax.axis_index("row")
    col = lax.axis_index("col")
    z, core = row // 2, row % 2
    y, x = col // NX, col % NX
    sib = (z * 2 + 1 - core, col)
    zpair = z + 1 - 2 * (z % 2)
    quad_same = (zpair * 2 + core, col)
    quad_diag = (zpair * 2 + 1 - core, col)

    def at_z(step):
        return (((z + step) % NZ) * 2 + core, col)

    def at_xy(dx, dy):
        return (row, ((y + dy) % NY) * NX + (x + dx) % NX)

    def remote(src, dst, ssem, rsem, dev):
        return pltpu.make_async_remote_copy(
            src_ref=src, dst_ref=dst, send_sem=ssem, recv_sem=rsem, device_id=dev, device_id_type=MESH
        )

    barrier = pltpu.get_barrier_semaphore()
    plane = [(o % NX, o // NX) for o in range(1, NX * NY)]
    partners = [at_z(step) for step in RING] + [at_xy(dx, dy) for dx, dy in plane] + [sib, quad_diag]
    for dev in partners:
        pl.semaphore_signal(barrier, inc=1, device_id=dev, device_id_type=MESH)

    load = pltpu.make_async_copy(a_ref.at[0, 0], a_buf, loc_sem)
    load.start()

    for i in range(4):
        pt[i] = p_ref[i].astype(F32).T.astype(BF16)
    lane8 = lax.broadcasted_iota(jnp.int32, (8, 128), 1)
    mine = jnp.zeros((8, 128), jnp.int32)
    for i in range(4):
        mine = jnp.where(lane8 == i, agg_ref[i], mine)
    agg_mine[...] = mine
    agg_quad[0] = mine
    d = (z + NZ - col) % NZ

    @pl.when(d == 0)
    def _():
        agg_col[core] = mine
        for t in range(2):
            p_buf[core * 2 + t] = jnp.concatenate([p_ref[2 * t], p_ref[2 * t + 1]], axis=1)

    load.wait()

    @pl.loop(0, 16)
    def _(s):
        live = s < count_ref[0, 0]
        left = jnp.dot(pt[rows_ref[0, 0, s]], a_buf[s], preferred_element_type=F32)
        left = jnp.where(live, left, 0.0)
        high = left.astype(BF16)
        lhl[s, 0:64] = high
        lhl[s, 64:128] = (left - high.astype(F32)).astype(BF16)

    pl.semaphore_wait(barrier, len(partners))

    in_tree = d == TREE[0]
    for step in TREE[1:]:
        in_tree = in_tree | (d == step)

    def own_half(t):
        return p_buf.at[core * 2 + t]

    def agg_copy(dev, ssem):
        return remote(agg_col.at[core], agg_col.at[core], ssem, ag_rsem, dev)

    def p_copy(t, dev, ssem):
        return remote(own_half(t), own_half(t), ssem, p_rsem.at[t], dev)

    quad_devs = (sib, quad_same, quad_diag)
    for k in range(3):
        remote(agg_mine, agg_quad.at[k + 1], q_ssem.at[k], q_rsem.at[k], quad_devs[k]).start()

    @pl.when(d == 0)
    def _():
        for k, step in enumerate(TREE):
            agg_copy(at_z(step), ag_ssem.at[k]).start()
        for t in range(2):
            for k, step in enumerate(TREE):
                p_copy(t, at_z(step), p_ssem.at[t, k]).start()

    @pl.when(d != 0)
    def _():
        agg_copy(at_z(1), ag_ssem.at[0]).wait_recv()

    @pl.when(in_tree)
    def _():
        for k, step in enumerate((1, 15)):
            agg_copy(at_z(step), af_ssem.at[k]).start()

    agg_sib = remote(agg_col.at[core], agg_col.at[core], as_ssem, as_rsem, sib)
    agg_sib.start()
    agg_sib_in = remote(agg_col.at[1 - core], agg_col.at[1 - core], as_ssem, as_rsem, sib)
    agg_sib_in.wait_recv()
    to_smem = pltpu.make_async_copy(agg_col, col_s, sm_sem)
    to_smem.start()
    to_smem.wait()

    for s in range(16):
        j = cols_ref[0, 0, s]
        key = rows_ref[0, 0, s] * 32 + col_s[j // 4, 0, j % 4]
        key_s[0, s] = jnp.where(s < count_ref[0, 0], key, -1)
    last = jnp.zeros((8, 128), jnp.int32)
    for s in range(16):
        before = jnp.int32(0)
        for o in range(s):
            before = jnp.where(key_s[0, o] == key_s[0, s], o + 1, before)
        key_s[1, s] = before
        last = jnp.where(lane8 == key_s[0, s], s + 1, last)
    last_vec[...] = last
    to_smem = pltpu.make_async_copy(last_vec, last_s, sm_sem)
    to_smem.start()
    to_smem.wait()

    run[0] = jnp.zeros((64, 128), F32)

    for t in range(2):
        @pl.when(d != 0)
        def _():
            p_copy(t, at_z(1), p_ssem.at[t, 0]).wait_recv()

        @pl.when(in_tree)
        def _():
            for k, step in enumerate((1, 15)):
                p_copy(t, at_z(step), f_ssem.at[t, k]).start()

        remote(own_half(t), own_half(t), sib_ssem.at[t], sib_rsem.at[t], sib).start()
    for t in range(2):
        other = p_buf.at[(1 - core) * 2 + t]
        remote(other, other, sib_ssem.at[t], sib_rsem.at[t], sib).wait_recv()

    lane = lax.broadcasted_iota(jnp.int32, (64, 128), 1)

    @pl.loop(0, 16)
    def _(s):
        j = cols_ref[0, 0, s]
        both = jnp.dot(lhl[s], p_buf[j // 2], preferred_element_type=F32)
        prod = both[0:64] + both[64:128]
        turned = pltpu.roll(prod, 64, 1)
        keep = (lane // 64) == (j % 2)
        run[s + 1] = jnp.where(keep, prod, turned) + run[key_s[1, s]]

    @pl.loop(0, 64)
    def _(t):
        i, yy, xx = t // 16, (t // 4) % 4, t % 4
        base = i * 32 + (t % 16) * 2
        block = jnp.where(lane < 64, run[last_s[0, base]], run[last_s[0, base + 1]])
        d_a[xx, yy, i] = block[0:32]
        d_b[yy, xx, i] = block[32:64]

    first = []
    for k in range(1, 4):
        first.append(remote(d_a.at[(x + k) % NX], r_a.at[k - 1], x_ssem.at[0, k - 1], x_rsem.at[0, k - 1], at_xy(k, 0)))
        first.append(remote(d_b.at[(y + k) % NY], r_b.at[k - 1], x_ssem.at[1, k - 1], x_rsem.at[1, k - 1], at_xy(0, k)))
    for copy in first:
        copy.start()
    for copy in first:
        copy.wait_recv()
    for dense, got, total, here in ((d_a, r_a, e_a, x), (d_b, r_b, e_b, y)):
        @pl.loop(0, 4)
        def _(o):
            total[o] = (dense[here, o] + got[0, o]) + (got[1, o] + got[2, o])

    second = []
    for k in range(1, 4):
        second.append(remote(e_a.at[(y + k) % NY], r2_a.at[k - 1], x2_ssem.at[0, k - 1], x2_rsem.at[0, k - 1], at_xy(0, k)))
        second.append(remote(e_b.at[(x + k) % NX], r2_b.at[k - 1], x2_ssem.at[1, k - 1], x2_rsem.at[1, k - 1], at_xy(k, 0)))
    for copy in second:
        copy.start()
    for copy in second:
        copy.wait_recv()
    quad[0, :, 0:32] = (e_a[y] + r2_a[0]) + (r2_a[1] + r2_a[2])
    quad[0, :, 32:64] = (e_b[x] + r2_b[0]) + (r2_b[1] + r2_b[2])

    to_sib = remote(quad.at[0], quad.at[1], z_ssem.at[0], z_rsem.at[0], sib)
    to_pair = remote(quad.at[0], quad.at[2], z_ssem.at[1], z_rsem.at[1], quad_same)
    on_sib = remote(quad.at[2], quad.at[3], z_ssem.at[2], z_rsem.at[2], sib)
    to_pair.start()
    to_sib.start()

    for k in range(3):
        remote(agg_mine, agg_quad.at[k + 1], q_ssem.at[k], q_rsem.at[k], quad_devs[k]).wait()
    to_smem = pltpu.make_async_copy(agg_quad, quad_s, sm_sem)
    to_smem.start()
    to_smem.wait()
    labels = [quad_s[g // 4, 0, g % 4] for g in range(16)]

    run_z[0] = jnp.zeros((64, 128), F32)

    def chain(group):
        for g in range(group * 4, group * 4 + 4):
            before = jnp.int32(0)
            for o in range(g):
                before = jnp.where(labels[o] == labels[g], o + 1, before)
            run_z[g + 1] = quad[group, g % 4] + run_z[before]

    chain(0)
    to_sib.wait_recv()
    chain(1)
    to_pair.wait_recv()
    on_sib.start()
    chain(2)
    on_sib.wait_recv()
    chain(3)

    far = []
    for k, step in enumerate((0,) + FAR):
        wanted = relay_ref[((z + step) % NZ) * 2 + core]
        at = jnp.int32(0)
        for g in range(16):
            at = jnp.where(labels[g] == wanted, g + 1, at)
        ob[k] = run_z[at]
        if k:
            copy = remote(ob.at[k], rz.at[k - 1], w_ssem.at[k - 1], w_rsem.at[k - 1], at_z(step))
            copy.start()
            far.append(copy)
    total = ob[0]
    for k, copy in enumerate(far):
        copy.wait_recv()
        total = total + rz[k]
    tile[...] = total

    spread = []
    for k, (dx, dy) in enumerate(plane):
        copy = remote(tile, gat.at[k], o_ssem.at[k], o_rsem.at[k], at_xy(dx, dy))
        copy.start()
        spread.append(copy)
    out_ref[0, :, pl.ds(pl.multiple_of(col * 128, 128), 128)] = tile[...]
    for k, (dx, dy) in enumerate(plane):
        spread[k].wait_recv()
        source = ((y + NY - dy) % NY) * NX + (x + NX - dx) % NX
        out_ref[0, :, pl.ds(pl.multiple_of(source * 128, 128), 128)] = gat[k]

    for copy in first + second + [to_sib, to_pair, on_sib] + far + spread + [agg_sib]:
        copy.wait_send()
    for t in range(2):
        remote(own_half(t), own_half(t), sib_ssem.at[t], sib_rsem.at[t], sib).wait_send()

    @pl.when(d == 0)
    def _():
        for k, step in enumerate(TREE):
            agg_copy(at_z(step), ag_ssem.at[k]).wait_send()
            for t in range(2):
                p_copy(t, at_z(step), p_ssem.at[t, k]).wait_send()

    @pl.when(in_tree)
    def _():
        for k, step in enumerate((1, 15)):
            agg_copy(at_z(step), af_ssem.at[k]).wait_send()
            for t in range(2):
                p_copy(t, at_z(step), f_ssem.at[t, k]).wait_send()


def on_device(a_blocks, slot_row, slot_col, slot_count, p_blocks, aggregate, relayout):
    smem = pl.BlockSpec(memory_space=pltpu.SMEM)
    vmem = pl.BlockSpec(memory_space=pltpu.VMEM)
    dma = pltpu.SemaphoreType.DMA
    return pl.pallas_call(
        kernel,
        out_shape=jax.ShapeDtypeStruct((1, 64, 2048), F32),
        in_specs=[pl.BlockSpec(memory_space=pl.ANY), smem, smem, smem, vmem, smem, smem],
        out_specs=vmem,
        scratch_shapes=[
            pltpu.VMEM((16, 320, 320), BF16),
            pltpu.VMEM((4, 64, 320), BF16),
            pltpu.VMEM((16, 128, 320), BF16),
            pltpu.VMEM((4, 320, 128), BF16),
            pltpu.VMEM((8, 128), jnp.int32),
            pltpu.VMEM((2, 8, 128), jnp.int32),
            pltpu.VMEM((4, 8, 128), jnp.int32),
            pltpu.VMEM((8, 128), jnp.int32),
            pltpu.SMEM((2, 8, 128), jnp.int32),
            pltpu.SMEM((4, 8, 128), jnp.int32),
            pltpu.SMEM((8, 128), jnp.int32),
            pltpu.SMEM((2, 16), jnp.int32),
            pltpu.VMEM((17, 64, 128), F32),
            pltpu.VMEM((4, 4, 4, 32, 128), F32),
            pltpu.VMEM((4, 4, 4, 32, 128), F32),
            pltpu.VMEM((3, 4, 4, 32, 128), F32),
            pltpu.VMEM((3, 4, 4, 32, 128), F32),
            pltpu.VMEM((4, 4, 32, 128), F32),
            pltpu.VMEM((4, 4, 32, 128), F32),
            pltpu.VMEM((3, 4, 32, 128), F32),
            pltpu.VMEM((3, 4, 32, 128), F32),
            pltpu.VMEM((4, 4, 64, 128), F32),
            pltpu.VMEM((17, 64, 128), F32),
            pltpu.VMEM((8, 64, 128), F32),
            pltpu.VMEM((7, 64, 128), F32),
            pltpu.VMEM((64, 128), F32),
            pltpu.VMEM((15, 64, 128), F32),
            dma, dma,
            dma((2, 5)), dma((2,)), dma((2, 2)), dma((2,)), dma((2,)),
            dma((5,)), dma, dma((2,)), dma, dma,
            dma((3,)), dma((3,)),
            dma((2, 3)), dma((2, 3)), dma((2, 3)), dma((2, 3)),
            dma((3,)), dma((3,)), dma((7,)), dma((7,)), dma((15,)), dma((15,)),
        ],
        compiler_params=pltpu.CompilerParams(
            collective_id=0, has_side_effects=True, vmem_limit_bytes=40 << 20
        ),
        name="coarse_operator",
    )(a_blocks, slot_row, slot_col, slot_count, p_blocks, aggregate, relayout)


def solution(mesh):
    return jax.shard_map(
        on_device,
        mesh=mesh,
        in_specs=(
            P("row", "col", None, None, None),
            P("row", "col", None),
            P("row", "col", None),
            P("row", "col"),
            P("row", None, None),
            P("row"),
            P(),
        ),
        out_specs=P("row", None, None),
        check_vma=False,
    )
```

time: 429 us -> 98.1 us (0.23)
  waiting for transfers between devices: 324 us -> 0 us
  Pallas kernels: 0 us -> 89.2 us
  blocking collectives: 44.3 us -> 0 us
  matrix products: 23.4 us -> 0 us
  between operations: 16.5 us -> 0.68 us
  local copies, waits for them, and re-layouts: 14 us -> 6.67 us
    reduce_scatter x2 -> x0, waiting for transfers between devices: 196 us -> none  [the longest x1 108 us: on_device(): owned = lax.psum_scatter(stacked, 'row', scatter_dimension=0, tiled=True)]
    all_gather x2 -> x0, waiting for transfers between devices: 127 us -> none  [the longest x1 72.5 us: on_device(): gathered = lax.all_gather(owned, 'row', axis=0, tiled=True)]
    pallas_call x0 -> x1, Pallas kernels: none -> 89.2 us  [on_device(): pl.pallas_call(kernel, out_shape=jax.ShapeDtypeStruct((1, 64, 2048), F32)...]
    unnamed x1 -> x0, blocking collectives: 24.4 us -> none
    dot_general x4 -> x0, matrix products: 23.4 us -> none  [the longest x1 10.2 us: on_device(): applied = jnp.einsum('isq,sak->iaqk', weights, products, precision=highest)]
    all_gather x1 -> x0, blocking collectives: 19.8 us -> none  [on_device(): return lax.all_gather(flattened, 'col', axis=2, tiled=True)]
    transpose x2 -> x0, local copies, waits for them, and re-layouts: 5.3 us -> none  [the longest x1 5.25 us: on_device(): jnp.einsum('iam,iaqk->iqmk', p_blocks.astype(jnp.float32), applied, preci...]
  transfers between devices with their start and end apart: 4 -> 0, of which waited for: 4 -> 0; matrix products, arithmetic and copies ran while one was open for 1% -> 0% of each run, Pallas kernels for 0% -> 0%
where the time goes in v1:
time: 98.1 us; the launch traced here: 96.6 us
  Pallas kernels  89.2 us (91%)
  local copies, waits for them, and re-layouts  6.67 us (7%)
    pallas_call x1, Pallas kernels, on_device(): pl.pallas_call(kernel, out_shape=jax.ShapeDtypeStruct((1, 64, 2048), F32)...  89.2 us
    unnamed x12, local copies, waits for them, and re-layouts  6.67 us

profile of v1, /device:TPU:1, one launch (start us, length us, event | category | flops | bytes accessed | tf_op | source)
XLA Modules:
  0.0 96.6 jit_solution(10684347666695519273)
XLA Ops:
  0.7 1.1 %copy.8.p_ref = bf16[4,320,64]{2,1,0:T(8,128)(2,1)S(1)} copy(bf16[4,320,64]{1,2,0:T(8,128)(2,1)} %param.11) | data formatting | bytes 327680 | tf_op args[4]
  1.8 0.0 copy-start
  1.8 2.1 %copy-done = bf16[1,1,16,320,320]{4,3,2,1,0:T(8,128)(2,1)S(1)} copy-done((bf16[1,1,16,320,320]{4,3,2,1,0:T(8,128)(2,1)S(1)}, bf16[1,1,16,320,320]{4,3,2,1,0:T(8,128)(2,1)}, u32[]{:S(2)}) %copy-start) | copy-done | bytes 3276824
  3.9 0.0 copy-start.1
  3.9 0.7 copy-done.1
  4.6 0.0 copy-start.2
  4.6 0.7 copy-done.2
  5.2 0.0 copy-start.3
  5.2 0.7 copy-done.3
  5.9 0.0 copy-start.4
  5.9 0.7 copy-done.4
  6.5 89.2 %coarse_operator.1 = f32[1,64,2048]{2,1,0:T(8,128)S(1)} custom-call(bf16[1,1,16,320,320]{4,3,2,1,0:T(8,128)(2,1)S(1)} %copy-done, s32[1,1,16]{2,1,0:T(1,128)S(1)} %copy-done.1, s32[1,1,16]{2,1,0:T(1,128)S(1)} %copy-done.2, s32[1,1]{1,0:T(1,128)S(6)} %copy.10.count_ref, bf16[4,320,64]{2,1,0:T(8,128)(2,1)S(1)} %copy.8.p_ref, s32[4]{0:T(128)S(1)} %copy-done.3, ...), custom_call_target="tpu_custom_call" | custom-call | tf_op jit(solution)/shard_map/coarse_operator/pallas_call | solution.py:286
  95.8 0.8 copy.11
Async XLA Ops:
  1.8 2.1 %copy-start = (bf16[1,1,16,320,320]{4,3,2,1,0:T(8,128)(2,1)S(1)}, bf16[1,1,16,320,320]{4,3,2,1,0:T(8,128)(2,1)}, u32[]{:S(2)}) copy-start(bf16[1,1,16,320,320]{4,3,2,1,0:T(8,128)(2,1)} %a_ref.1) | copy-start | bytes 9830404
  3.9 0.7 copy-start.1
  4.6 0.7 copy-start.2
  5.2 0.7 copy-start.3
  5.9 0.7 copy-start.4

commit v2 on v1

v2 whole, which is shorter than its diff:
```python
import functools

import jax
import jax.numpy as jnp
from jax import lax
from jax.experimental import pallas as pl
from jax.experimental.pallas import tpu as pltpu
from jax.sharding import PartitionSpec as P

MESH = pl.DeviceIdType.MESH

NX, NY, NZ = 4, 4, 16
TREE = (8, 5, 11, 2, 14)
FAR = (2, 14, 4, 12, 6, 10, 8)
RING = (1, 15, 2, 14, 4, 12, 5, 11, 6, 10, 8)
F32 = jnp.float32
BF16 = jnp.bfloat16


def kernel(
    a_hbm, rows_hbm, cols_hbm, count_hbm, p_ref, agg_hbm, relay_hbm, out_ref,
    a_buf, lhl, p_buf, rows_ref, cols_ref, count_ref, agg_ref, relay_ref,
    agg_mine, agg_col, agg_quad, keys_x, keys_y, table, col_s, quad_s, table_s,
    g_a, g_b, run_a, run_b, e_a, e_b, r2_a, r2_b, quad, run_z, ob, rz, tile, gat,
    loc_sem, sm_sem, p_ssem, p_rsem, f_ssem, sib_ssem, sib_rsem, ag_ssem, ag_rsem, af_ssem, as_ssem, as_rsem,
    q_ssem, q_rsem, k_ssem, k_rsem, x_ssem, x_rsem, x2_ssem, x2_rsem, z_ssem, z_rsem, w_ssem, w_rsem, o_ssem, o_rsem,
):
    row = lax.axis_index("row")
    col = lax.axis_index("col")
    z, core = row // 2, row % 2
    y, x = col // NX, col % NX
    sib = (z * 2 + 1 - core, col)
    zpair = z + 1 - 2 * (z % 2)
    quad_same = (zpair * 2 + core, col)
    quad_diag = (zpair * 2 + 1 - core, col)
    pending = []

    def at_z(step):
        return (((z + step) % NZ) * 2 + core, col)

    def at_xy(dx, dy):
        return (row, ((y + dy) % NY) * NX + (x + dx) % NX)

    def remote(src, dst, ssem, rsem, dev):
        return pltpu.make_async_remote_copy(
            src_ref=src, dst_ref=dst, send_sem=ssem, recv_sem=rsem, device_id=dev, device_id_type=MESH
        )

    def start(copy):
        copy.start()
        pending.append(copy.wait_send)
        return copy

    def finish():
        for wait in pending:
            wait()

    barrier = pltpu.get_barrier_semaphore()
    plane = [(o % NX, o // NX) for o in range(1, NX * NY)]
    partners = [at_z(step) for step in RING] + [at_xy(dx, dy) for dx, dy in plane] + [sib, quad_diag]
    for dev in partners:
        pl.semaphore_signal(barrier, inc=1, device_id=dev, device_id_type=MESH)

    small = ((rows_hbm, rows_ref), (cols_hbm, cols_ref), (count_hbm, count_ref), (agg_hbm, agg_ref), (relay_hbm, relay_ref))
    loads = [pltpu.make_async_copy(src, dst, loc_sem.at[k]) for k, (src, dst) in enumerate(small)]
    loads.append(pltpu.make_async_copy(a_hbm.at[0, 0], a_buf, loc_sem.at[5]))
    for load in loads:
        load.start()
    for load in loads[:5]:
        load.wait()

    lane8 = lax.broadcasted_iota(jnp.int32, (8, 128), 1)
    mine = jnp.zeros((8, 128), jnp.int32)
    for i in range(4):
        mine = jnp.where(lane8 == i, agg_ref[i], mine)
    agg_mine[...] = mine
    agg_quad[0] = mine
    d = (z + NZ - col) % NZ

    @pl.when(d == 0)
    def _():
        agg_col[core] = mine
        for t in range(2):
            both = jnp.concatenate([p_ref[2 * t], p_ref[2 * t + 1]], axis=0)
            p_buf[core * 2 + t] = both.astype(F32).T.astype(BF16)

    loads[5].wait()

    @pl.loop(0, 16)
    def _(s):
        live = s < count_ref[0, 0]
        left = jnp.dot(p_ref[rows_ref[0, 0, s]], a_buf[s], preferred_element_type=F32)
        left = jnp.where(live, left, 0.0)
        high = left.astype(BF16)
        lhl[s, 0:64] = high
        lhl[s, 64:128] = (left - high.astype(F32)).astype(BF16)

    pl.semaphore_wait(barrier, len(partners))

    in_tree = d == TREE[0]
    for step in TREE[1:]:
        in_tree = in_tree | (d == step)

    def own_half(t):
        return p_buf.at[core * 2 + t]

    def agg_copy(dev, ssem):
        return remote(agg_col.at[core], agg_col.at[core], ssem, ag_rsem, dev)

    def p_copy(t, dev, ssem):
        return remote(own_half(t), own_half(t), ssem, p_rsem.at[t], dev)

    def start_when(condition, copies):
        @pl.when(condition)
        def _():
            for copy in copies:
                copy.start()

        def wait():
            @pl.when(condition)
            def _():
                for copy in copies:
                    copy.wait_send()

        pending.append(wait)

    quad_devs = (sib, quad_same, quad_diag)
    quad_in = [start(remote(agg_mine, agg_quad.at[k + 1], q_ssem.at[k], q_rsem.at[k], quad_devs[k])) for k in range(3)]
    start_when(d == 0, [agg_copy(at_z(step), ag_ssem.at[k]) for k, step in enumerate(TREE)])
    for t in range(2):
        start_when(d == 0, [p_copy(t, at_z(step), p_ssem.at[t, k]) for k, step in enumerate(TREE)])

    @pl.when(d != 0)
    def _():
        agg_copy(at_z(1), ag_ssem.at[0]).wait_recv()

    start_when(in_tree, [agg_copy(at_z(step), af_ssem.at[k]) for k, step in enumerate((1, 15))])
    start(remote(agg_col.at[core], agg_col.at[core], as_ssem, as_rsem, sib))
    for t in range(2):
        @pl.when(d != 0)
        def _():
            p_copy(t, at_z(1), p_ssem.at[t, 0]).wait_recv()

        start_when(in_tree, [p_copy(t, at_z(step), f_ssem.at[t, k]) for k, step in enumerate((1, 15))])
        start(remote(own_half(t), own_half(t), sib_ssem.at[t], sib_rsem.at[t], sib))

    remote(agg_col.at[1 - core], agg_col.at[1 - core], as_ssem, as_rsem, sib).wait_recv()
    to_smem = pltpu.make_async_copy(agg_col, col_s, sm_sem)
    to_smem.start()
    to_smem.wait()
    for s in range(16):
        j = cols_ref[0, 0, s]
        key = rows_ref[0, 0, s] * 32 + col_s[j // 4, 0, j % 4]
        line = jnp.full((1, 128), jnp.where(s < count_ref[0, 0], key, -1), jnp.int32)
        keys_x[0, s : s + 1] = line
        keys_y[0, s : s + 1] = line
    keys_in = []
    for k in range(1, 4):
        keys_in.append(start(remote(keys_x.at[0], keys_x.at[k], k_ssem.at[0, k - 1], k_rsem.at[0, k - 1], at_xy(k, 0))))
        keys_in.append(start(remote(keys_y.at[0], keys_y.at[k], k_ssem.at[1, k - 1], k_rsem.at[1, k - 1], at_xy(0, k))))

    for t in range(2):
        other = p_buf.at[(1 - core) * 2 + t]
        remote(other, other, sib_ssem.at[t], sib_rsem.at[t], sib).wait_recv()

    lane = lax.broadcasted_iota(jnp.int32, (64, 128), 1)

    def product(s, side):
        j = cols_ref[0, 0, s]
        both = jnp.dot(lhl[s], p_buf[j // 2], preferred_element_type=F32)
        prod = both[0:64] + both[64:128]
        return jnp.where(j % 2 == side, prod, pltpu.roll(prod, 64, 1))

    @pl.loop(0, 8)
    def _(t):
        pair = jnp.where(lane < 64, product(2 * t, 0), product(2 * t + 1, 1))
        g_a[0, t] = pair[0:32]
        g_b[0, t] = pair[32:64]

    first_a, first_b = [], []
    for k in range(1, 4):
        first_a.append(start(remote(g_a.at[0], g_a.at[k], x_ssem.at[0, k - 1], x_rsem.at[0, k - 1], at_xy(k, 0))))
        first_b.append(start(remote(g_b.at[0], g_b.at[k], x_ssem.at[1, k - 1], x_rsem.at[1, k - 1], at_xy(0, k))))

    for copy in keys_in:
        copy.wait_recv()
    lane_i = lax.broadcasted_iota(jnp.int32, (64, 128), 1)
    slot_i = lax.broadcasted_iota(jnp.int32, (64, 128), 0)
    table[...] = jnp.zeros((8, 128), jnp.int32)
    for h, keys in enumerate((keys_x, keys_y)):
        down = keys[...].reshape(64, 128)
        across = jnp.sum(jnp.where(slot_i == lane_i, down, 0), axis=0, keepdims=True)
        before = jnp.where((down == across) & (slot_i < lane_i), slot_i + 1, 0)
        table[2 * h : 2 * h + 1] = jnp.max(before, axis=0, keepdims=True)
        table[2 * h + 1 : 2 * h + 2] = jnp.max(jnp.where(down == lane_i, slot_i + 1, 0), axis=0, keepdims=True)
    to_smem = pltpu.make_async_copy(table, table_s, sm_sem)
    to_smem.start()
    to_smem.wait()

    half_lane = lax.broadcasted_iota(jnp.int32, (32, 128), 1)
    low = half_lane < 64
    run_a[0] = jnp.zeros((32, 128), F32)
    run_b[0] = jnp.zeros((32, 128), F32)
    for k in range(4):
        if k:
            first_a[k - 1].wait_recv()
            first_b[k - 1].wait_recv()

        @pl.loop(0, 8)
        def _(t):
            for h, (got, run) in enumerate(((g_a, run_a), (g_b, run_b))):
                pair = got[k, t]
                turned = pltpu.roll(pair, 64, 1)
                s = k * 16 + 2 * t
                run[s + 1] = jnp.where(low, pair, turned) + run[table_s[2 * h, s]]
                run[s + 2] = jnp.where(low, turned, pair) + run[table_s[2 * h, s + 1]]

    second_a, second_b = [], []
    for k in (1, 2, 3, 0):
        there = (y + k) % NY
        for i in range(4):
            at = i * 32 + (there * NX + x) * 2
            e_a[k, i] = jnp.where(low, run_a[table_s[1, at]], run_a[table_s[1, at + 1]])
        if k:
            second_a.append(start(remote(e_a.at[k], r2_a.at[k - 1], x2_ssem.at[0, k - 1], x2_rsem.at[0, k - 1], at_xy(0, k))))
        there = (x + k) % NX
        for i in range(4):
            at = i * 32 + (y * NX + there) * 2
            e_b[k, i] = jnp.where(low, run_b[table_s[3, at]], run_b[table_s[3, at + 1]])
        if k:
            second_b.append(start(remote(e_b.at[k], r2_b.at[k - 1], x2_ssem.at[1, k - 1], x2_rsem.at[1, k - 1], at_xy(k, 0))))

    to_pair, to_sib, on_sib = [], [], []
    for h, (second, own, got) in enumerate(((second_a, e_a, r2_a), (second_b, e_b, r2_b))):
        for copy in second:
            copy.wait_recv()
        quad[0, h] = (own[0] + got[0]) + (got[1] + got[2])
        to_pair.append(start(remote(quad.at[0, h], quad.at[2, h], z_ssem.at[h, 1], z_rsem.at[h, 1], quad_same)))
        to_sib.append(start(remote(quad.at[0, h], quad.at[1, h], z_ssem.at[h, 0], z_rsem.at[h, 0], sib)))
        on_sib.append(remote(quad.at[2, h], quad.at[3, h], z_ssem.at[h, 2], z_rsem.at[h, 2], sib))

    for copy in quad_in:
        copy.wait_recv()
    to_smem = pltpu.make_async_copy(agg_quad, quad_s, sm_sem)
    to_smem.start()
    to_smem.wait()
    labels = [quad_s[g // 4, 0, g % 4] for g in range(16)]
    previous = []
    for g in range(16):
        before = jnp.int32(0)
        for o in range(g):
            before = jnp.where(labels[o] == labels[g], o + 1, before)
        previous.append(before)
    lasts = []
    for step in (0,) + FAR:
        wanted = relay_ref[((z + step) % NZ) * 2 + core]
        at = jnp.int32(0)
        for g in range(16):
            at = jnp.where(labels[g] == wanted, g + 1, at)
        lasts.append(at)

    def chain(h, group):
        for g in range(group * 4, group * 4 + 4):
            run_z[h, g + 1] = quad[group, h, g % 4] + run_z[h, previous[g]]

    for h in range(2):
        run_z[h, 0] = jnp.zeros((32, 128), F32)
        chain(h, 0)
    for h in range(2):
        to_pair[h].wait_recv()
        start(on_sib[h])
    for h in range(2):
        to_sib[h].wait_recv()
        chain(h, 1)
        chain(h, 2)

    far = ([], [])
    for h in range(2):
        on_sib[h].wait_recv()
        chain(h, 3)
        for k, step in enumerate((0,) + FAR):
            ob[h, k] = run_z[h, lasts[k]]
            if k:
                far[h].append(start(remote(ob.at[h, k], rz.at[h, k - 1], w_ssem.at[h, k - 1], w_rsem.at[h, k - 1], at_z(step))))

    spread = ([], [])
    for h in range(2):
        total = ob[h, 0]
        for k, copy in enumerate(far[h]):
            copy.wait_recv()
            total = total + rz[h, k]
        tile[h] = total
        for k, (dx, dy) in enumerate(plane):
            spread[h].append(start(remote(tile.at[h], gat.at[h, k], o_ssem.at[h, k], o_rsem.at[h, k], at_xy(dx, dy))))
        out_ref[0, 32 * h : 32 * h + 32, pl.ds(pl.multiple_of(col * 128, 128), 128)] = tile[h]
    for h in range(2):
        for k, (dx, dy) in enumerate(plane):
            spread[h][k].wait_recv()
            source = ((y + NY - dy) % NY) * NX + (x + NX - dx) % NX
            out_ref[0, 32 * h : 32 * h + 32, pl.ds(pl.multiple_of(source * 128, 128), 128)] = gat[h, k]
    finish()


def on_device(a_blocks, slot_row, slot_col, slot_count, p_blocks, aggregate, relayout):
    hbm = pl.BlockSpec(memory_space=pltpu.HBM)
    vmem = pl.BlockSpec(memory_space=pltpu.VMEM)
    dma = pltpu.SemaphoreType.DMA
    return pl.pallas_call(
        kernel,
        out_shape=jax.ShapeDtypeStruct((1, 64, 2048), F32),
        in_specs=[hbm, hbm, hbm, hbm, vmem, hbm, hbm],
        out_specs=vmem,
        scratch_shapes=[
            pltpu.VMEM((16, 320, 320), BF16),
            pltpu.VMEM((16, 128, 320), BF16),
            pltpu.VMEM((4, 320, 128), BF16),
            pltpu.SMEM((1, 1, 16), jnp.int32),
            pltpu.SMEM((1, 1, 16), jnp.int32),
            pltpu.SMEM((1, 1), jnp.int32),
            pltpu.SMEM((4,), jnp.int32),
            pltpu.SMEM((32,), jnp.int32),
            pltpu.VMEM((8, 128), jnp.int32),
            pltpu.VMEM((2, 8, 128), jnp.int32),
            pltpu.VMEM((4, 8, 128), jnp.int32),
            pltpu.VMEM((4, 16, 128), jnp.int32),
            pltpu.VMEM((4, 16, 128), jnp.int32),
            pltpu.VMEM((8, 128), jnp.int32),
            pltpu.SMEM((2, 8, 128), jnp.int32),
            pltpu.SMEM((4, 8, 128), jnp.int32),
            pltpu.SMEM((8, 128), jnp.int32),
            pltpu.VMEM((4, 8, 32, 128), F32),
            pltpu.VMEM((4, 8, 32, 128), F32),
            pltpu.VMEM((65, 32, 128), F32),
            pltpu.VMEM((65, 32, 128), F32),
            pltpu.VMEM((4, 4, 32, 128), F32),
            pltpu.VMEM((4, 4, 32, 128), F32),
            pltpu.VMEM((3, 4, 32, 128), F32),
            pltpu.VMEM((3, 4, 32, 128), F32),
            pltpu.VMEM((4, 2, 4, 32, 128), F32),
            pltpu.VMEM((2, 17, 32, 128), F32),
            pltpu.VMEM((2, 8, 32, 128), F32),
            pltpu.VMEM((2, 7, 32, 128), F32),
            pltpu.VMEM((2, 32, 128), F32),
            pltpu.VMEM((2, 15, 32, 128), F32),
            dma((6,)), dma,
            dma((2, 5)), dma((2,)), dma((2, 2)), dma((2,)), dma((2,)),
            dma((5,)), dma, dma((2,)), dma, dma,
            dma((3,)), dma((3,)), dma((2, 3)), dma((2, 3)),
            dma((2, 3)), dma((2, 3)), dma((2, 3)), dma((2, 3)),
            dma((2, 3)), dma((2, 3)), dma((2, 7)), dma((2, 7)), dma((2, 15)), dma((2, 15)),
        ],
        compiler_params=pltpu.CompilerParams(
            collective_id=0, has_side_effects=True, vmem_limit_bytes=60 << 20
        ),
        name="coarse_operator",
    )(a_blocks, slot_row, slot_col, slot_count, jnp.swapaxes(p_blocks, 1, 2), aggregate, relayout)


def solution(mesh):
    return jax.shard_map(
        on_device,
        mesh=mesh,
        in_specs=(
            P("row", "col", None, None, None),
            P("row", "col", None),
            P("row", "col", None),
            P("row", "col"),
            P("row", None, None),
            P("row"),
            P(),
        ),
        out_specs=P("row", None, None),
        check_vma=False,
    )
```

time: 98.1 us -> 85.5 us (0.87); the launches traced: 96.6 us -> 85.3 us
  Pallas kernels: 89.2 us -> 82.7 us
  local copies, waits for them, and re-layouts: 6.67 us -> 1.87 us
    pallas_call x1, Pallas kernels: 89.2 us -> 82.7 us  [on_device(): pl.pallas_call(kernel, out_shape=jax.ShapeDtypeStruct((1, 64, 2048), F32)...]
    unnamed x12 -> x1, local copies, waits for them, and re-layouts: 6.67 us -> 1.87 us
where the time goes in v2:
time: 85.5 us; the launch traced here: 85.3 us
  Pallas kernels  82.7 us (97%)
  local copies, waits for them, and re-layouts  1.87 us (2%)
    pallas_call x1, Pallas kernels, on_device(): pl.pallas_call(kernel, out_shape=jax.ShapeDtypeStruct((1, 64, 2048), F32)...  82.7 us
    unnamed x1, local copies, waits for them, and re-layouts  1.87 us

profile of v2, /device:TPU:1, one launch (start us, length us, event | category | flops | bytes accessed | tf_op | source)
XLA Modules:
  0.0 85.3 jit_solution(11465422715949576879)
XLA Ops:
  0.7 82.7 %coarse_operator.1 = f32[1,64,2048]{2,1,0:T(8,128)} custom-call(bf16[1,1,16,320,320]{4,3,2,1,0:T(8,128)(2,1)} %a_hbm.1, s32[1,1,16]{2,1,0:T(1,128)} %rows_hbm.1, s32[1,1,16]{2,1,0:T(1,128)} %cols_hbm.1, s32[1,1]{1,0:T(1,128)S(6)} %copy.9.count_hbm, bf16[4,64,320]{2,1,0:T(8,128)(2,1)} %bitcast.1, s32[4]{0:T(128)} %agg_hbm.1, s32[32]{0:T(128)} %relay_hbm.1), custom_call_target="tpu_custom_call" | custom-call | tf_op jit(solution)/shard_map/coarse_operator/pallas_call | solution.py:308
  83.4 1.9 %copy.10 = f32[1,64,2048]{2,1,0:T(8,128)} copy(f32[1,64,2048]{2,1,0:T(8,128)} %coarse_operator.1) | data formatting | bytes 1048576

commit v3 on v2

--- a/solution.py
+++ b/solution.py
@@ -19,7 +19,7 @@
 
 def kernel(
     a_hbm, rows_hbm, cols_hbm, count_hbm, p_ref, agg_hbm, relay_hbm, out_ref,
-    a_buf, lhl, p_buf, rows_ref, cols_ref, count_ref, agg_ref, relay_ref,
+    a_buf, lhl, p_buf0, p_buf1, rows_ref, cols_ref, count_ref, agg_ref, relay_ref,
     agg_mine, agg_col, agg_quad, keys_x, keys_y, table, col_s, quad_s, table_s,
     g_a, g_b, run_a, run_b, e_a, e_b, r2_a, r2_b, quad, run_z, ob, rz, tile, gat,
     loc_sem, sm_sem, p_ssem, p_rsem, f_ssem, sib_ssem, sib_rsem, ag_ssem, ag_rsem, af_ssem, as_ssem, as_rsem,
@@ -34,6 +34,7 @@
     quad_same = (zpair * 2 + core, col)
     quad_diag = (zpair * 2 + 1 - core, col)
     pending = []
+    p_buf = (p_buf0, p_buf1)
 
     def at_z(step):
         return (((z + step) % NZ) * 2 + core, col)
@@ -81,8 +82,43 @@
     def _():
         agg_col[core] = mine
         for t in range(2):
-            both = jnp.concatenate([p_ref[2 * t], p_ref[2 * t + 1]], axis=0)
-            p_buf[core * 2 + t] = both.astype(F32).T.astype(BF16)
+            both = jnp.concatenate([p_ref[i, 32 * t : 32 * t + 32] for i in range(4)], axis=0)
+            p_buf[t][core] = both.astype(F32).T.astype(BF16)
+
+    pl.semaphore_wait(barrier, len(partners))
+
+    in_tree = d == TREE[0]
+    for step in TREE[1:]:
+        in_tree = in_tree | (d == step)
+
+    def own_half(t):
+        return p_buf[t].at[core]
+
+    def agg_copy(dev, ssem):
+        return remote(agg_col.at[core], agg_col.at[core], ssem, ag_rsem, dev)
+
+    def p_copy(t, dev, ssem):
+        return remote(own_half(t), own_half(t), ssem, p_rsem.at[t], dev)
+
+    def start_when(condition, copies):
+        @pl.when(condition)
+        def _():
+            for copy in copies:
+                copy.start()
+
+        def wait():
+            @pl.when(condition)
+            def _():
+                for copy in copies:
+                    copy.wait_send()
+
+        pending.append(wait)
+
+    quad_devs = (sib, quad_same, quad_diag)
+    quad_in = [start(remote(agg_mine, agg_quad.at[k + 1], q_ssem.at[k], q_rsem.at[k], quad_devs[k])) for k in range(3)]
+    start_when(d == 0, [agg_copy(at_z(step), ag_ssem.at[k]) for k, step in enumerate(TREE)])
+    for t in range(2):
+        start_when(d == 0, [p_copy(t, at_z(step), p_ssem.at[t, k]) for k, step in enumerate(TREE)])
 
     loads[5].wait()
 
@@ -95,54 +131,12 @@
         lhl[s, 0:64] = high
         lhl[s, 64:128] = (left - high.astype(F32)).astype(BF16)
 
-    pl.semaphore_wait(barrier, len(partners))
-
-    in_tree = d == TREE[0]
-    for step in TREE[1:]:
-        in_tree = in_tree | (d == step)
-
-    def own_half(t):
-        return p_buf.at[core * 2 + t]
-
-    def agg_copy(dev, ssem):
-        return remote(agg_col.at[core], agg_col.at[core], ssem, ag_rsem, dev)
-
-    def p_copy(t, dev, ssem):
-        return remote(own_half(t), own_half(t), ssem, p_rsem.at[t], dev)
-
-    def start_when(condition, copies):
-        @pl.when(condition)
-        def _():
-            for copy in copies:
-                copy.start()
-
-        def wait():
-            @pl.when(condition)
-            def _():
-                for copy in copies:
-                    copy.wait_send()
-
-        pending.append(wait)
-
-    quad_devs = (sib, quad_same, quad_diag)
-    quad_in = [start(remote(agg_mine, agg_quad.at[k + 1], q_ssem.at[k], q_rsem.at[k], quad_devs[k])) for k in range(3)]
-    start_when(d == 0, [agg_copy(at_z(step), ag_ssem.at[k]) for k, step in enumerate(TREE)])
-    for t in range(2):
-        start_when(d == 0, [p_copy(t, at_z(step), p_ssem.at[t, k]) for k, step in enumerate(TREE)])
-
     @pl.when(d != 0)
     def _():
         agg_copy(at_z(1), ag_ssem.at[0]).wait_recv()
 
     start_when(in_tree, [agg_copy(at_z(step), af_ssem.at[k]) for k, step in enumerate((1, 15))])
     start(remote(agg_col.at[core], agg_col.at[core], as_ssem, as_rsem, sib))
-    for t in range(2):
-        @pl.when(d != 0)
-        def _():
-            p_copy(t, at_z(1), p_ssem.at[t, 0]).wait_recv()
-
-        start_when(in_tree, [p_copy(t, at_z(step), f_ssem.at[t, k]) for k, step in enumerate((1, 15))])
-        start(remote(own_half(t), own_half(t), sib_ssem.at[t], sib_rsem.at[t], sib))
 
     remote(agg_col.at[1 - core], agg_col.at[1 - core], as_ssem, as_rsem, sib).wait_recv()
     to_smem = pltpu.make_async_copy(agg_col, col_s, sm_sem)
@@ -159,28 +153,42 @@
         keys_in.append(start(remote(keys_x.at[0], keys_x.at[k], k_ssem.at[0, k - 1], k_rsem.at[0, k - 1], at_xy(k, 0))))
         keys_in.append(start(remote(keys_y.at[0], keys_y.at[k], k_ssem.at[1, k - 1], k_rsem.at[1, k - 1], at_xy(0, k))))
 
-    for t in range(2):
-        other = p_buf.at[(1 - core) * 2 + t]
+    group = lax.broadcasted_iota(jnp.int32, (64, 128), 1) // 32
+    small_group = lax.broadcasted_iota(jnp.int32, (32, 128), 1) // 32
+    low = small_group < 2
+
+    def prolongator_in(t):
+        @pl.when(d != 0)
+        def _():
+            p_copy(t, at_z(1), p_ssem.at[t, 0]).wait_recv()
+
+        start_when(in_tree, [p_copy(t, at_z(step), f_ssem.at[t, k]) for k, step in enumerate((1, 15))])
+        start(remote(own_half(t), own_half(t), sib_ssem.at[t], sib_rsem.at[t], sib))
+        other = p_buf[t].at[1 - core]
         remote(other, other, sib_ssem.at[t], sib_rsem.at[t], sib).wait_recv()
 
-    lane = lax.broadcasted_iota(jnp.int32, (64, 128), 1)
-
-    def product(s, side):
+    def product(t, s, v):
         j = cols_ref[0, 0, s]
-        both = jnp.dot(lhl[s], p_buf[j // 2], preferred_element_type=F32)
-        prod = both[0:64] + both[64:128]
-        return jnp.where(j % 2 == side, prod, pltpu.roll(prod, 64, 1))
-
-    @pl.loop(0, 8)
-    def _(t):
-        pair = jnp.where(lane < 64, product(2 * t, 0), product(2 * t + 1, 1))
-        g_a[0, t] = pair[0:32]
-        g_b[0, t] = pair[32:64]
-
-    first_a, first_b = [], []
-    for k in range(1, 4):
-        first_a.append(start(remote(g_a.at[0], g_a.at[k], x_ssem.at[0, k - 1], x_rsem.at[0, k - 1], at_xy(k, 0))))
-        first_b.append(start(remote(g_b.at[0], g_b.at[k], x_ssem.at[1, k - 1], x_rsem.at[1, k - 1], at_xy(0, k))))
+        both = jnp.dot(lhl[s], p_buf[t][j // 4], preferred_element_type=F32)
+        return pltpu.roll(both[0:64] + both[64:128], ((v + 4 - j % 4) % 4) * 32, 1)
+
+    first_a, first_b = ([], []), ([], [])
+
+    def products_out(t):
+        @pl.loop(0, 4)
+        def _(u):
+            four = product(t, 4 * u, 0)
+            for v in range(1, 4):
+                four = jnp.where(group == v, product(t, 4 * u + v, v), four)
+            g_a[t, 0, u] = four[0:32]
+            g_b[t, 0, u] = four[32:64]
+
+        for k in range(1, 4):
+            first_a[t].append(start(remote(g_a.at[t, 0], g_a.at[t, k], x_ssem.at[t, 0, k - 1], x_rsem.at[t, 0, k - 1], at_xy(k, 0))))
+            first_b[t].append(start(remote(g_b.at[t, 0], g_b.at[t, k], x_ssem.at[t, 1, k - 1], x_rsem.at[t, 1, k - 1], at_xy(0, k))))
+
+    prolongator_in(0)
+    products_out(0)
 
     for copy in keys_in:
         copy.wait_recv()
@@ -195,46 +203,61 @@
         table[2 * h + 1 : 2 * h + 2] = jnp.max(jnp.where(down == lane_i, slot_i + 1, 0), axis=0, keepdims=True)
     to_smem = pltpu.make_async_copy(table, table_s, sm_sem)
     to_smem.start()
+
+    prolongator_in(1)
+    products_out(1)
     to_smem.wait()
 
-    half_lane = lax.broadcasted_iota(jnp.int32, (32, 128), 1)
-    low = half_lane < 64
     run_a[0] = jnp.zeros((32, 128), F32)
     run_b[0] = jnp.zeros((32, 128), F32)
-    for k in range(4):
-        if k:
-            first_a[k - 1].wait_recv()
-            first_b[k - 1].wait_recv()
-
-        @pl.loop(0, 8)
-        def _(t):
-            for h, (got, run) in enumerate(((g_a, run_a), (g_b, run_b))):
-                pair = got[k, t]
-                turned = pltpu.roll(pair, 64, 1)
-                s = k * 16 + 2 * t
-                run[s + 1] = jnp.where(low, pair, turned) + run[table_s[2 * h, s]]
-                run[s + 2] = jnp.where(low, turned, pair) + run[table_s[2 * h, s + 1]]
-
-    second_a, second_b = [], []
-    for k in (1, 2, 3, 0):
-        there = (y + k) % NY
-        for i in range(4):
-            at = i * 32 + (there * NX + x) * 2
-            e_a[k, i] = jnp.where(low, run_a[table_s[1, at]], run_a[table_s[1, at + 1]])
-        if k:
-            second_a.append(start(remote(e_a.at[k], r2_a.at[k - 1], x2_ssem.at[0, k - 1], x2_rsem.at[0, k - 1], at_xy(0, k))))
-        there = (x + k) % NX
-        for i in range(4):
-            at = i * 32 + (y * NX + there) * 2
-            e_b[k, i] = jnp.where(low, run_b[table_s[3, at]], run_b[table_s[3, at + 1]])
-        if k:
-            second_b.append(start(remote(e_b.at[k], r2_b.at[k - 1], x2_ssem.at[1, k - 1], x2_rsem.at[1, k - 1], at_xy(k, 0))))
+    second_a, second_b = ([], []), ([], [])
+
+    def blocks(run, h, first_key):
+        parts = [run[table_s[2 * h + 1, first_key + o]] for o in (0, 1, 32, 33)]
+        return jnp.where(
+            low, jnp.where(small_group == 0, parts[0], parts[1]), jnp.where(small_group == 2, parts[2], parts[3])
+        )
+
+    def sums_out(t):
+        for k in range(4):
+            if k:
+                first_a[t][k - 1].wait_recv()
+                first_b[t][k - 1].wait_recv()
+
+            @pl.loop(0, 4)
+            def _(u):
+                for v in range(4):
+                    s = k * 16 + 4 * u + v
+                    for h, (got, run) in enumerate(((g_a, run_a), (g_b, run_b))):
+                        one = jnp.where(small_group == v, got[t, k, u], 0.0)
+                        one = one + pltpu.roll(one, 64, 1)
+                        one = one + pltpu.roll(one, 32, 1)
+                        run[s + 1] = one + run[table_s[2 * h, s]]
+
+        for k in (1, 2, 3, 0):
+            there = ((y + k) % NY) * NX + x
+            for n in range(2):
+                e_a[t, k, n] = blocks(run_a, 0, n * 64 + there * 2)
+            if k:
+                second_a[t].append(start(remote(e_a.at[t, k], r2_a.at[t, k - 1], x2_ssem.at[t, 0, k - 1], x2_rsem.at[t, 0, k - 1], at_xy(0, k))))
+            there = y * NX + (x + k) % NX
+            for n in range(2):
+                e_b[t, k, n] = blocks(run_b, 1, n * 64 + there * 2)
+            if k:
+                second_b[t].append(start(remote(e_b.at[t, k], r2_b.at[t, k - 1], x2_ssem.at[t, 1, k - 1], x2_rsem.at[t, 1, k - 1], at_xy(k, 0))))
+
+    sums_out(0)
+    sums_out(1)
 
     to_pair, to_sib, on_sib = [], [], []
-    for h, (second, own, got) in enumerate(((second_a, e_a, r2_a), (second_b, e_b, r2_b))):
-        for copy in second:
+    for h in range(2):
+        for copy in second_a[h] + second_b[h]:
             copy.wait_recv()
-        quad[0, h] = (own[0] + got[0]) + (got[1] + got[2])
+        for n in range(2):
+            top = (e_a[h, 0, n] + r2_a[h, 0, n]) + (r2_a[h, 1, n] + r2_a[h, 2, n])
+            bottom = (e_b[h, 0, n] + r2_b[h, 0, n]) + (r2_b[h, 1, n] + r2_b[h, 2, n])
+            quad[0, h, 2 * n] = jnp.where(low, top, pltpu.roll(bottom, 64, 1))
+            quad[0, h, 2 * n + 1] = jnp.where(low, pltpu.roll(top, 64, 1), bottom)
         to_pair.append(start(remote(quad.at[0, h], quad.at[2, h], z_ssem.at[h, 1], z_rsem.at[h, 1], quad_same)))
         to_sib.append(start(remote(quad.at[0, h], quad.at[1, h], z_ssem.at[h, 0], z_rsem.at[h, 0], sib)))
         on_sib.append(remote(quad.at[2, h], quad.at[3, h], z_ssem.at[h, 2], z_rsem.at[h, 2], sib))
@@ -292,12 +315,27 @@
         tile[h] = total
         for k, (dx, dy) in enumerate(plane):
             spread[h].append(start(remote(tile.at[h], gat.at[h, k], o_ssem.at[h, k], o_rsem.at[h, k], at_xy(dx, dy))))
-        out_ref[0, 32 * h : 32 * h + 32, pl.ds(pl.multiple_of(col * 128, 128), 128)] = tile[h]
-    for h in range(2):
-        for k, (dx, dy) in enumerate(plane):
-            spread[h][k].wait_recv()
-            source = ((y + NY - dy) % NY) * NX + (x + NX - dx) % NX
-            out_ref[0, 32 * h : 32 * h + 32, pl.ds(pl.multiple_of(source * 128, 128), 128)] = gat[h, k]
+
+    def place(source, first, second):
+        there = pl.ds(pl.multiple_of(source * 128, 128), 128)
+        out_ref[0, 0:32, there] = jnp.where(
+            low,
+            jnp.where(small_group == 0, first, pltpu.roll(second, 32, 1)),
+            jnp.where(small_group == 2, pltpu.roll(first, 32, 1), pltpu.roll(second, 64, 1)),
+        )
+        out_ref[0, 32:64, there] = jnp.where(
+            low,
+            jnp.where(small_group == 0, pltpu.roll(first, 64, 1), pltpu.roll(second, 96, 1)),
+            jnp.where(small_group == 2, pltpu.roll(first, 96, 1), second),
+        )
+
+    place(col, tile[0], tile[1])
+    for copy in spread[0]:
+        copy.wait_recv()
+    for k, (dx, dy) in enumerate(plane):
+        spread[1][k].wait_recv()
+        source = ((y + NY - dy) % NY) * NX + (x + NX - dx) % NX
+        place(source, gat[0, k], gat[1, k])
     finish()
 
 
@@ -307,13 +345,14 @@
     dma = pltpu.SemaphoreType.DMA
     return pl.pallas_call(
         kernel,
-        out_shape=jax.ShapeDtypeStruct((1, 64, 2048), F32),
+        out_shape=pltpu.VMEM((1, 64, 2048), F32),
         in_specs=[hbm, hbm, hbm, hbm, vmem, hbm, hbm],
         out_specs=vmem,
         scratch_shapes=[
             pltpu.VMEM((16, 320, 320), BF16),
             pltpu.VMEM((16, 128, 320), BF16),
-            pltpu.VMEM((4, 320, 128), BF16),
+            pltpu.VMEM((2, 320, 128), BF16),
+            pltpu.VMEM((2, 320, 128), BF16),
             pltpu.SMEM((1, 1, 16), jnp.int32),
             pltpu.SMEM((1, 1, 16), jnp.int32),
             pltpu.SMEM((1, 1), jnp.int32),
@@ -328,14 +367,14 @@
             pltpu.SMEM((2, 8, 128), jnp.int32),
             pltpu.SMEM((4, 8, 128), jnp.int32),
             pltpu.SMEM((8, 128), jnp.int32),
-            pltpu.VMEM((4, 8, 32, 128), F32),
-            pltpu.VMEM((4, 8, 32, 128), F32),
+            pltpu.VMEM((2, 4, 4, 32, 128), F32),
+            pltpu.VMEM((2, 4, 4, 32, 128), F32),
             pltpu.VMEM((65, 32, 128), F32),
             pltpu.VMEM((65, 32, 128), F32),
-            pltpu.VMEM((4, 4, 32, 128), F32),
-            pltpu.VMEM((4, 4, 32, 128), F32),
-            pltpu.VMEM((3, 4, 32, 128), F32),
-            pltpu.VMEM((3, 4, 32, 128), F32),
+            pltpu.VMEM((2, 4, 2, 32, 128), F32),
+            pltpu.VMEM((2, 4, 2, 32, 128), F32),
+            pltpu.VMEM((2, 3, 2, 32, 128), F32),
+            pltpu.VMEM((2, 3, 2, 32, 128), F32),
             pltpu.VMEM((4, 2, 4, 32, 128), F32),
             pltpu.VMEM((2, 17, 32, 128), F32),
             pltpu.VMEM((2, 8, 32, 128), F32),
@@ -346,7 +385,7 @@
             dma((2, 5)), dma((2,)), dma((2, 2)), dma((2,)), dma((2,)),
             dma((5,)), dma, dma((2,)), dma, dma,
             dma((3,)), dma((3,)), dma((2, 3)), dma((2, 3)),
-            dma((2, 3)), dma((2, 3)), dma((2, 3)), dma((2, 3)),
+            dma((2, 2, 3)), dma((2, 2, 3)), dma((2, 2, 3)), dma((2, 2, 3)),
             dma((2, 3)), dma((2, 3)), dma((2, 7)), dma((2, 7)), dma((2, 15)), dma((2, 15)),
         ],
         compiler_params=pltpu.CompilerParams(

time: 85.5 us -> 79 us (0.924)
  Pallas kernels: 82.7 us -> 77.2 us
  local copies, waits for them, and re-layouts: 1.87 us -> 0.8 us
    pallas_call x1, Pallas kernels: 82.7 us -> 77.2 us  [on_device(): pl.pallas_call(kernel, out_shape=pltpu.VMEM((1, 64, 2048), F32), in_specs...]
    unnamed x1, local copies, waits for them, and re-layouts: 1.87 us -> 0.8 us
where the time goes in v3:
time: 79 us; the launch traced here: 78.7 us
  Pallas kernels  77.2 us (98%)
  local copies, waits for them, and re-layouts  0.8 us (1%)
    pallas_call x1, Pallas kernels, on_device(): pl.pallas_call(kernel, out_shape=pltpu.VMEM((1, 64, 2048), F32), in_specs...  77.2 us

profile of v3, /device:TPU:1, one launch (start us, length us, event | category | flops | bytes accessed | tf_op | source)
XLA Modules:
  0.0 78.7 jit_solution(7429239695055417090)
XLA Ops:
  0.7 77.2 %coarse_operator.1 = f32[1,64,2048]{2,1,0:T(8,128)S(1)} custom-call(bf16[1,1,16,320,320]{4,3,2,1,0:T(8,128)(2,1)} %a_hbm.1, s32[1,1,16]{2,1,0:T(1,128)} %rows_hbm.1, s32[1,1,16]{2,1,0:T(1,128)} %cols_hbm.1, s32[1,1]{1,0:T(1,128)S(6)} %copy.10.count_hbm, bf16[4,64,320]{2,1,0:T(8,128)(2,1)} %bitcast.1, s32[4]{0:T(128)} %agg_hbm.1, s32[32]{0:T(128)} %relay_hbm.1), custom_call_target="tpu_custom_call" | custom-call | tf_op jit(solution)/shard_map/coarse_operator/pallas_call | solution.py:346
  77.9 0.8 %copy.9 = f32[1,64,2048]{2,1,0:T(8,128)} copy(f32[1,64,2048]{2,1,0:T(8,128)S(1)} %coarse_operator.1) | data formatting | bytes 1048576

commit v4 on v3

--- a/solution.py
+++ b/solution.py
@@ -10,9 +10,9 @@
 MESH = pl.DeviceIdType.MESH
 
 NX, NY, NZ = 4, 4, 16
-TREE = (8, 5, 11, 2, 14)
+TREE = (6, 10, 2, 14)
 FAR = (2, 14, 4, 12, 6, 10, 8)
-RING = (1, 15, 2, 14, 4, 12, 5, 11, 6, 10, 8)
+RING = (1, 15, 2, 14, 4, 12, 6, 10, 8)
 F32 = jnp.float32
 BF16 = jnp.bfloat16
 
@@ -114,11 +114,20 @@
 
         pending.append(wait)
 
+    def pass_on(copy_to):
+        start_when((d == 6) | (d == 10), [copy_to(2, 0)])
+        start_when(d == 6, [copy_to(14, 1)])
+        start_when(in_tree, [copy_to(1, 2), copy_to(15, 3)])
+
     quad_devs = (sib, quad_same, quad_diag)
     quad_in = [start(remote(agg_mine, agg_quad.at[k + 1], q_ssem.at[k], q_rsem.at[k], quad_devs[k])) for k in range(3)]
     start_when(d == 0, [agg_copy(at_z(step), ag_ssem.at[k]) for k, step in enumerate(TREE)])
-    for t in range(2):
-        start_when(d == 0, [p_copy(t, at_z(step), p_ssem.at[t, k]) for k, step in enumerate(TREE)])
+    p_out = [[p_copy(t, at_z(step), p_ssem.at[t, k]) for k, step in enumerate(TREE)] for t in range(2)]
+
+    @pl.when(d == 0)
+    def _():
+        for copy in p_out[0]:
+            copy.start()
 
     loads[5].wait()
 
@@ -131,41 +140,71 @@
         lhl[s, 0:64] = high
         lhl[s, 64:128] = (left - high.astype(F32)).astype(BF16)
 
+    @pl.when(d == 0)
+    def _():
+        for copy in p_out[0]:
+            copy.wait_send()
+
+    start_when(d == 0, p_out[1])
+
     @pl.when(d != 0)
     def _():
         agg_copy(at_z(1), ag_ssem.at[0]).wait_recv()
 
-    start_when(in_tree, [agg_copy(at_z(step), af_ssem.at[k]) for k, step in enumerate((1, 15))])
+    pass_on(lambda step, k: agg_copy(at_z(step), af_ssem.at[k]))
     start(remote(agg_col.at[core], agg_col.at[core], as_ssem, as_rsem, sib))
 
-    remote(agg_col.at[1 - core], agg_col.at[1 - core], as_ssem, as_rsem, sib).wait_recv()
-    to_smem = pltpu.make_async_copy(agg_col, col_s, sm_sem)
-    to_smem.start()
-    to_smem.wait()
-    for s in range(16):
-        j = cols_ref[0, 0, s]
-        key = rows_ref[0, 0, s] * 32 + col_s[j // 4, 0, j % 4]
-        line = jnp.full((1, 128), jnp.where(s < count_ref[0, 0], key, -1), jnp.int32)
-        keys_x[0, s : s + 1] = line
-        keys_y[0, s : s + 1] = line
     keys_in = []
     for k in range(1, 4):
-        keys_in.append(start(remote(keys_x.at[0], keys_x.at[k], k_ssem.at[0, k - 1], k_rsem.at[0, k - 1], at_xy(k, 0))))
-        keys_in.append(start(remote(keys_y.at[0], keys_y.at[k], k_ssem.at[1, k - 1], k_rsem.at[1, k - 1], at_xy(0, k))))
+        keys_in.append(remote(keys_x.at[0], keys_x.at[k], k_ssem.at[0, k - 1], k_rsem.at[0, k - 1], at_xy(k, 0)))
+        keys_in.append(remote(keys_y.at[0], keys_y.at[k], k_ssem.at[1, k - 1], k_rsem.at[1, k - 1], at_xy(0, k)))
+    for copy in keys_in:
+        pending.append(copy.wait_send)
+
+    def keys_out():
+        remote(agg_col.at[1 - core], agg_col.at[1 - core], as_ssem, as_rsem, sib).wait_recv()
+        to_smem = pltpu.make_async_copy(agg_col, col_s, sm_sem)
+        to_smem.start()
+        to_smem.wait()
+        for s in range(16):
+            j = cols_ref[0, 0, s]
+            key = rows_ref[0, 0, s] * 32 + col_s[j // 4, 0, j % 4]
+            line = jnp.full((1, 128), jnp.where(s < count_ref[0, 0], key, -1), jnp.int32)
+            keys_x[0, s : s + 1] = line
+            keys_y[0, s : s + 1] = line
+        for copy in keys_in:
+            copy.start()
+
+    outside = (d != 0) & jnp.logical_not(in_tree)
+
+    @pl.when(jnp.logical_not(in_tree))
+    def _():
+        keys_out()
+
+    @pl.when(d != 0)
+    def _():
+        p_copy(0, at_z(1), p_ssem.at[0, 0]).wait_recv()
+
+    pass_on(lambda step, k: p_copy(0, at_z(step), f_ssem.at[0, k]))
+    start(remote(own_half(0), own_half(0), sib_ssem.at[0], sib_rsem.at[0], sib))
+
+    @pl.when(in_tree)
+    def _():
+        p_copy(1, at_z(1), p_ssem.at[1, 0]).wait_recv()
+
+    pass_on(lambda step, k: p_copy(1, at_z(step), f_ssem.at[1, k]))
+
+    @pl.when(in_tree)
+    def _():
+        keys_out()
+
+    def sibling_in(t):
+        other = p_buf[t].at[1 - core]
+        remote(other, other, sib_ssem.at[t], sib_rsem.at[t], sib).wait_recv()
 
     group = lax.broadcasted_iota(jnp.int32, (64, 128), 1) // 32
     small_group = lax.broadcasted_iota(jnp.int32, (32, 128), 1) // 32
     low = small_group < 2
-
-    def prolongator_in(t):
-        @pl.when(d != 0)
-        def _():
-            p_copy(t, at_z(1), p_ssem.at[t, 0]).wait_recv()
-
-        start_when(in_tree, [p_copy(t, at_z(step), f_ssem.at[t, k]) for k, step in enumerate((1, 15))])
-        start(remote(own_half(t), own_half(t), sib_ssem.at[t], sib_rsem.at[t], sib))
-        other = p_buf[t].at[1 - core]
-        remote(other, other, sib_ssem.at[t], sib_rsem.at[t], sib).wait_recv()
 
     def product(t, s, v):
         j = cols_ref[0, 0, s]
@@ -187,8 +226,14 @@
             first_a[t].append(start(remote(g_a.at[t, 0], g_a.at[t, k], x_ssem.at[t, 0, k - 1], x_rsem.at[t, 0, k - 1], at_xy(k, 0))))
             first_b[t].append(start(remote(g_b.at[t, 0], g_b.at[t, k], x_ssem.at[t, 1, k - 1], x_rsem.at[t, 1, k - 1], at_xy(0, k))))
 
-    prolongator_in(0)
+    sibling_in(0)
     products_out(0)
+
+    @pl.when(outside)
+    def _():
+        p_copy(1, at_z(1), p_ssem.at[1, 0]).wait_recv()
+
+    start(remote(own_half(1), own_half(1), sib_ssem.at[1], sib_rsem.at[1], sib))
 
     for copy in keys_in:
         copy.wait_recv()
@@ -204,7 +249,7 @@
     to_smem = pltpu.make_async_copy(table, table_s, sm_sem)
     to_smem.start()
 
-    prolongator_in(1)
+    sibling_in(1)
     products_out(1)
     to_smem.wait()
 
@@ -382,8 +427,8 @@
             pltpu.VMEM((2, 32, 128), F32),
             pltpu.VMEM((2, 15, 32, 128), F32),
             dma((6,)), dma,
-            dma((2, 5)), dma((2,)), dma((2, 2)), dma((2,)), dma((2,)),
-            dma((5,)), dma, dma((2,)), dma, dma,
+            dma((2, 4)), dma((2,)), dma((2, 4)), dma((2,)), dma((2,)),
+            dma((4,)), dma, dma((4,)), dma, dma,
             dma((3,)), dma((3,)), dma((2, 3)), dma((2, 3)),
             dma((2, 2, 3)), dma((2, 2, 3)), dma((2, 2, 3)), dma((2, 2, 3)),
             dma((2, 3)), dma((2, 3)), dma((2, 7)), dma((2, 7)), dma((2, 15)), dma((2, 15)),

time: 79 us -> 73.8 us (0.934); the launches traced: 78.7 us -> 72.6 us
  Pallas kernels: 77.2 us -> 71.1 us
    pallas_call x1, Pallas kernels: 77.2 us -> 71.1 us  [on_device(): pl.pallas_call(kernel, out_shape=pltpu.VMEM((1, 64, 2048), F32), in_specs...]
where the time goes in v4:
time: 73.8 us; the launch traced here: 72.6 us
  Pallas kernels  71.1 us (96%)
  local copies, waits for them, and re-layouts  0.8 us (1%)
    pallas_call x1, Pallas kernels, on_device(): pl.pallas_call(kernel, out_shape=pltpu.VMEM((1, 64, 2048), F32), in_specs...  71.1 us

profile of v4, /device:TPU:1, one launch (start us, length us, event | category | flops | bytes accessed | tf_op | source)
XLA Modules:
  0.0 72.6 jit_solution(11419127987645927980)
XLA Ops:
  0.7 71.1 %coarse_operator.1 = f32[1,64,2048]{2,1,0:T(8,128)S(1)} custom-call(bf16[1,1,16,320,320]{4,3,2,1,0:T(8,128)(2,1)} %a_hbm.1, s32[1,1,16]{2,1,0:T(1,128)} %rows_hbm.1, s32[1,1,16]{2,1,0:T(1,128)} %cols_hbm.1, s32[1,1]{1,0:T(1,128)S(6)} %copy.10.count_hbm, bf16[4,64,320]{2,1,0:T(8,128)(2,1)} %bitcast.1, s32[4]{0:T(128)} %agg_hbm.1, s32[32]{0:T(128)} %relay_hbm.1), custom_call_target="tpu_custom_call" | custom-call | tf_op jit(solution)/shard_map/coarse_operator/pallas_call | solution.py:391
  71.8 0.8 %copy.9 = f32[1,64,2048]{2,1,0:T(8,128)} copy(f32[1,64,2048]{2,1,0:T(8,128)S(1)} %coarse_operator.1) | data formatting | bytes 1048576

commit v5 on v4

--- a/solution.py
+++ b/solution.py
@@ -11,8 +11,9 @@
 
 NX, NY, NZ = 4, 4, 16
 TREE = (6, 10, 2, 14)
-FAR = (2, 14, 4, 12, 6, 10, 8)
+FAR = (8, 6, 10, 4, 12, 2, 14)
 RING = (1, 15, 2, 14, 4, 12, 6, 10, 8)
+STEPS = 32767.0
 F32 = jnp.float32
 BF16 = jnp.bfloat16
 
@@ -20,10 +21,10 @@
 def kernel(
     a_hbm, rows_hbm, cols_hbm, count_hbm, p_ref, agg_hbm, relay_hbm, out_ref,
     a_buf, lhl, p_buf0, p_buf1, rows_ref, cols_ref, count_ref, agg_ref, relay_ref,
-    agg_mine, agg_col, agg_quad, keys_x, keys_y, table, col_s, quad_s, table_s,
-    g_a, g_b, run_a, run_b, e_a, e_b, r2_a, r2_b, quad, run_z, ob, rz, tile, gat,
+    agg_mine, agg_col, agg_quad, keys_x, keys_y, table, col_s, quad_s, table_s, rows_s,
+    g_a, g_b, run_a, run_b, e_a, e_b, r2_a, r2_b, quad, run_z, own, ob, rz, scale, scale_in, tile, gat,
     loc_sem, sm_sem, p_ssem, p_rsem, f_ssem, sib_ssem, sib_rsem, ag_ssem, ag_rsem, af_ssem, as_ssem, as_rsem,
-    q_ssem, q_rsem, k_ssem, k_rsem, x_ssem, x_rsem, x2_ssem, x2_rsem, z_ssem, z_rsem, w_ssem, w_rsem, o_ssem, o_rsem,
+    q_ssem, q_rsem, k_ssem, k_rsem, x_ssem, x_rsem, x2_ssem, x2_rsem, z_ssem, z_rsem, w_ssem, w_rsem, v_ssem, v_rsem, o_ssem, o_rsem,
 ):
     row = lax.axis_index("row")
     col = lax.axis_index("col")
@@ -57,7 +58,7 @@
             wait()
 
     barrier = pltpu.get_barrier_semaphore()
-    plane = [(o % NX, o // NX) for o in range(1, NX * NY)]
+    plane = sorted(((o % NX, o // NX) for o in range(1, NX * NY)), key=lambda o: -min(o[0], NX - o[0]) - min(o[1], NY - o[1]))
     partners = [at_z(step) for step in RING] + [at_xy(dx, dy) for dx, dy in plane] + [sib, quad_diag]
     for dev in partners:
         pl.semaphore_signal(barrier, inc=1, device_id=dev, device_id_type=MESH)
@@ -131,8 +132,7 @@
 
     loads[5].wait()
 
-    @pl.loop(0, 16)
-    def _(s):
+    def left_product(s):
         live = s < count_ref[0, 0]
         left = jnp.dot(p_ref[rows_ref[0, 0, s]], a_buf[s], preferred_element_type=F32)
         left = jnp.where(live, left, 0.0)
@@ -140,12 +140,35 @@
         lhl[s, 0:64] = high
         lhl[s, 64:128] = (left - high.astype(F32)).astype(BF16)
 
+    pl.loop(0, 8)(left_product)
+
     @pl.when(d == 0)
     def _():
         for copy in p_out[0]:
             copy.wait_send()
 
     start_when(d == 0, p_out[1])
+
+    pl.loop(8, 16)(left_product)
+
+    for copy in quad_in:
+        copy.wait_recv()
+    to_smem = pltpu.make_async_copy(agg_quad, quad_s, sm_sem)
+    to_smem.start()
+    to_smem.wait()
+    labels = [quad_s[g // 4, 0, g % 4] for g in range(16)]
+    for g in range(16):
+        before = jnp.int32(0)
+        for o in range(g):
+            before = jnp.where(labels[o] == labels[g], o + 1, before)
+        rows_s[0, g] = before
+    for k, step in enumerate((0,) + FAR):
+        wanted = relay_ref[((z + step) % NZ) * 2 + core]
+        at = jnp.int32(0)
+        for g in range(16):
+            at = jnp.where(labels[g] == wanted, g + 1, at)
+        rows_s[1, k] = at
+
 
     @pl.when(d != 0)
     def _():
@@ -257,11 +280,12 @@
     run_b[0] = jnp.zeros((32, 128), F32)
     second_a, second_b = ([], []), ([], [])
 
+    def join(parts):
+        left = jnp.where(small_group == 0, parts[0], parts[1])
+        return jnp.where(low, left, jnp.where(small_group == 2, parts[2], parts[3]))
+
     def blocks(run, h, first_key):
-        parts = [run[table_s[2 * h + 1, first_key + o]] for o in (0, 1, 32, 33)]
-        return jnp.where(
-            low, jnp.where(small_group == 0, parts[0], parts[1]), jnp.where(small_group == 2, parts[2], parts[3])
-        )
+        return join([run[table_s[2 * h + 1, first_key + o]] for o in (0, 1, 32, 33)])
 
     def sums_out(t):
         for k in range(4):
@@ -271,13 +295,14 @@
 
             @pl.loop(0, 4)
             def _(u):
-                for v in range(4):
-                    s = k * 16 + 4 * u + v
-                    for h, (got, run) in enumerate(((g_a, run_a), (g_b, run_b))):
-                        one = jnp.where(small_group == v, got[t, k, u], 0.0)
-                        one = one + pltpu.roll(one, 64, 1)
-                        one = one + pltpu.roll(one, 32, 1)
-                        run[s + 1] = one + run[table_s[2 * h, s]]
+                for h, (got, run) in enumerate(((g_a, run_a), (g_b, run_b))):
+                    turned = [got[t, k, u]]
+                    for o in range(1, 4):
+                        turned.append(pltpu.roll(turned[0], 32 * o, 1))
+                    for v in range(4):
+                        s = k * 16 + 4 * u + v
+                        parts = [turned[(g + 4 - v) % 4] for g in range(4)]
+                        run[s + 1] = join(parts) + run[table_s[2 * h, s]]
 
         for k in (1, 2, 3, 0):
             there = ((y + k) % NY) * NX + x
@@ -307,56 +332,39 @@
         to_sib.append(start(remote(quad.at[0, h], quad.at[1, h], z_ssem.at[h, 0], z_rsem.at[h, 0], sib)))
         on_sib.append(remote(quad.at[2, h], quad.at[3, h], z_ssem.at[h, 2], z_rsem.at[h, 2], sib))
 
-    for copy in quad_in:
-        copy.wait_recv()
-    to_smem = pltpu.make_async_copy(agg_quad, quad_s, sm_sem)
-    to_smem.start()
-    to_smem.wait()
-    labels = [quad_s[g // 4, 0, g % 4] for g in range(16)]
-    previous = []
-    for g in range(16):
-        before = jnp.int32(0)
-        for o in range(g):
-            before = jnp.where(labels[o] == labels[g], o + 1, before)
-        previous.append(before)
-    lasts = []
-    for step in (0,) + FAR:
-        wanted = relay_ref[((z + step) % NZ) * 2 + core]
-        at = jnp.int32(0)
-        for g in range(16):
-            at = jnp.where(labels[g] == wanted, g + 1, at)
-        lasts.append(at)
-
     def chain(h, group):
         for g in range(group * 4, group * 4 + 4):
-            run_z[h, g + 1] = quad[group, h, g % 4] + run_z[h, previous[g]]
-
+            run_z[h, g + 1] = quad[group, h, g % 4] + run_z[h, rows_s[0, g]]
+
+    far, far_scale = ([], []), ([], [])
+    diagonal = lax.broadcasted_iota(jnp.int32, (32, 128), 0) == lax.broadcasted_iota(jnp.int32, (32, 128), 1)
     for h in range(2):
         run_z[h, 0] = jnp.zeros((32, 128), F32)
         chain(h, 0)
-    for h in range(2):
+        to_sib[h].wait_recv()
+        chain(h, 1)
         to_pair[h].wait_recv()
         start(on_sib[h])
-    for h in range(2):
-        to_sib[h].wait_recv()
-        chain(h, 1)
         chain(h, 2)
-
-    far = ([], [])
-    for h in range(2):
         on_sib[h].wait_recv()
         chain(h, 3)
-        for k, step in enumerate((0,) + FAR):
-            ob[h, k] = run_z[h, lasts[k]]
-            if k:
-                far[h].append(start(remote(ob.at[h, k], rz.at[h, k - 1], w_ssem.at[h, k - 1], w_rsem.at[h, k - 1], at_z(step))))
+        own[h] = run_z[h, rows_s[1, 0]]
+        for k, step in enumerate(FAR):
+            block = run_z[h, rows_s[1, k + 1]]
+            largest = jnp.maximum(jnp.max(jnp.abs(block), axis=1, keepdims=True), 1e-30)
+            ob[h, k] = jnp.round(block * (STEPS / largest)).astype(jnp.int32).astype(jnp.int16)
+            scale[h, k] = jnp.sum(jnp.where(diagonal, largest, 0.0), axis=0, keepdims=True)
+            far[h].append(start(remote(ob.at[h, k], rz.at[h, k], w_ssem.at[h, k], w_rsem.at[h, k], at_z(step))))
+            far_scale[h].append(start(remote(scale.at[h, k], scale_in.at[h, k], v_ssem.at[h, k], v_rsem.at[h, k], at_z(step))))
 
     spread = ([], [])
     for h in range(2):
-        total = ob[h, 0]
-        for k, copy in enumerate(far[h]):
-            copy.wait_recv()
-            total = total + rz[h, k]
+        total = own[h]
+        for k in range(len(FAR)):
+            far_scale[h][k].wait_recv()
+            largest = jnp.sum(jnp.where(diagonal, scale_in[h, k], 0.0), axis=1, keepdims=True)
+            far[h][k].wait_recv()
+            total = total + rz[h, k].astype(jnp.int32).astype(F32) * (largest / STEPS)
         tile[h] = total
         for k, (dx, dy) in enumerate(plane):
             spread[h].append(start(remote(tile.at[h], gat.at[h, k], o_ssem.at[h, k], o_rsem.at[h, k], at_xy(dx, dy))))
@@ -412,6 +420,7 @@
             pltpu.SMEM((2, 8, 128), jnp.int32),
             pltpu.SMEM((4, 8, 128), jnp.int32),
             pltpu.SMEM((8, 128), jnp.int32),
+            pltpu.SMEM((2, 16), jnp.int32),
             pltpu.VMEM((2, 4, 4, 32, 128), F32),
             pltpu.VMEM((2, 4, 4, 32, 128), F32),
             pltpu.VMEM((65, 32, 128), F32),
@@ -422,8 +431,11 @@
             pltpu.VMEM((2, 3, 2, 32, 128), F32),
             pltpu.VMEM((4, 2, 4, 32, 128), F32),
             pltpu.VMEM((2, 17, 32, 128), F32),
-            pltpu.VMEM((2, 8, 32, 128), F32),
-            pltpu.VMEM((2, 7, 32, 128), F32),
+            pltpu.VMEM((2, 32, 128), F32),
+            pltpu.VMEM((2, 7, 32, 128), jnp.int16),
+            pltpu.VMEM((2, 7, 32, 128), jnp.int16),
+            pltpu.VMEM((2, 7, 1, 128), F32),
+            pltpu.VMEM((2, 7, 1, 128), F32),
             pltpu.VMEM((2, 32, 128), F32),
             pltpu.VMEM((2, 15, 32, 128), F32),
             dma((6,)), dma,
@@ -431,7 +443,7 @@
             dma((4,)), dma, dma((4,)), dma, dma,
             dma((3,)), dma((3,)), dma((2, 3)), dma((2, 3)),
             dma((2, 2, 3)), dma((2, 2, 3)), dma((2, 2, 3)), dma((2, 2, 3)),
-            dma((2, 3)), dma((2, 3)), dma((2, 7)), dma((2, 7)), dma((2, 15)), dma((2, 15)),
+            dma((2, 3)), dma((2, 3)), dma((2, 7)), dma((2, 7)), dma((2, 7)), dma((2, 7)), dma((2, 15)), dma((2, 15)),
         ],
         compiler_params=pltpu.CompilerParams(
             collective_id=0, has_side_effects=True, vmem_limit_bytes=60 << 20

time: 73.8 us -> 69.6 us (0.943); the launches traced: 72.6 us -> 69.5 us
  Pallas kernels: 71.1 us -> 68 us
    pallas_call x1, Pallas kernels: 71.1 us -> 68 us  [on_device(): pl.pallas_call(kernel, out_shape=pltpu.VMEM((1, 64, 2048), F32), in_specs...]
where the time goes in v5:
time: 69.6 us; the launch traced here: 69.5 us
  Pallas kernels  68 us (98%)
  local copies, waits for them, and re-layouts  0.8 us (1%)
    pallas_call x1, Pallas kernels, on_device(): pl.pallas_call(kernel, out_shape=pltpu.VMEM((1, 64, 2048), F32), in_specs...  68 us

profile of v5, /device:TPU:1, one launch (start us, length us, event | category | flops | bytes accessed | tf_op | source)
XLA Modules:
  0.0 69.5 jit_solution(1468287009047060904)
XLA Ops:
  0.7 68.0 %coarse_operator.1 = f32[1,64,2048]{2,1,0:T(8,128)S(1)} custom-call(bf16[1,1,16,320,320]{4,3,2,1,0:T(8,128)(2,1)} %a_hbm.1, s32[1,1,16]{2,1,0:T(1,128)} %rows_hbm.1, s32[1,1,16]{2,1,0:T(1,128)} %cols_hbm.1, s32[1,1]{1,0:T(1,128)S(6)} %copy.10.count_hbm, bf16[4,64,320]{2,1,0:T(8,128)(2,1)} %bitcast.1, s32[4]{0:T(128)} %agg_hbm.1, s32[32]{0:T(128)} %relay_hbm.1), custom_call_target="tpu_custom_call" | custom-call | tf_op jit(solution)/shard_map/coarse_operator/pallas_call | solution.py:399
  68.7 0.8 %copy.9 = f32[1,64,2048]{2,1,0:T(8,128)} copy(f32[1,64,2048]{2,1,0:T(8,128)S(1)} %coarse_operator.1) | data formatting | bytes 1048576

commit v6 on v5

--- a/solution.py
+++ b/solution.py
@@ -12,7 +12,7 @@
 NX, NY, NZ = 4, 4, 16
 TREE = (6, 10, 2, 14)
 FAR = (8, 6, 10, 4, 12, 2, 14)
-RING = (1, 15, 2, 14, 4, 12, 6, 10, 8)
+RING = (6, 10, 4, 12, 2, 14, 1, 15)
 STEPS = 32767.0
 F32 = jnp.float32
 BF16 = jnp.bfloat16
@@ -23,7 +23,7 @@
     a_buf, lhl, p_buf0, p_buf1, rows_ref, cols_ref, count_ref, agg_ref, relay_ref,
     agg_mine, agg_col, agg_quad, keys_x, keys_y, table, col_s, quad_s, table_s, rows_s,
     g_a, g_b, run_a, run_b, e_a, e_b, r2_a, r2_b, quad, run_z, own, ob, rz, scale, scale_in, tile, gat,
-    loc_sem, sm_sem, p_ssem, p_rsem, f_ssem, sib_ssem, sib_rsem, ag_ssem, ag_rsem, af_ssem, as_ssem, as_rsem,
+    heard, loc_sem, sm_sem, p_ssem, p_rsem, f_ssem, sib_ssem, sib_rsem, ag_ssem, ag_rsem, af_ssem, as_ssem, as_rsem,
     q_ssem, q_rsem, k_ssem, k_rsem, x_ssem, x_rsem, x2_ssem, x2_rsem, z_ssem, z_rsem, w_ssem, w_rsem, v_ssem, v_rsem, o_ssem, o_rsem,
 ):
     row = lax.axis_index("row")
@@ -88,6 +88,9 @@
 
     pl.semaphore_wait(barrier, len(partners))
 
+    for step in (2, 14):
+        pl.semaphore_signal(heard, inc=1, device_id=at_z(step), device_id_type=MESH)
+
     in_tree = d == TREE[0]
     for step in TREE[1:]:
         in_tree = in_tree | (d == step)
@@ -121,7 +124,6 @@
         start_when(in_tree, [copy_to(1, 2), copy_to(15, 3)])
 
     quad_devs = (sib, quad_same, quad_diag)
-    quad_in = [start(remote(agg_mine, agg_quad.at[k + 1], q_ssem.at[k], q_rsem.at[k], quad_devs[k])) for k in range(3)]
     start_when(d == 0, [agg_copy(at_z(step), ag_ssem.at[k]) for k, step in enumerate(TREE)])
     p_out = [[p_copy(t, at_z(step), p_ssem.at[t, k]) for k, step in enumerate(TREE)] for t in range(2)]
 
@@ -129,6 +131,8 @@
     def _():
         for copy in p_out[0]:
             copy.start()
+
+    quad_in = [start(remote(agg_mine, agg_quad.at[k + 1], q_ssem.at[k], q_rsem.at[k], quad_devs[k])) for k in range(3)]
 
     loads[5].wait()
 
@@ -335,6 +339,8 @@
     def chain(h, group):
         for g in range(group * 4, group * 4 + 4):
             run_z[h, g + 1] = quad[group, h, g % 4] + run_z[h, rows_s[0, g]]
+
+    pl.semaphore_wait(heard, 2)
 
     far, far_scale = ([], []), ([], [])
     diagonal = lax.broadcasted_iota(jnp.int32, (32, 128), 0) == lax.broadcasted_iota(jnp.int32, (32, 128), 1)
@@ -438,7 +444,7 @@
             pltpu.VMEM((2, 7, 1, 128), F32),
             pltpu.VMEM((2, 32, 128), F32),
             pltpu.VMEM((2, 15, 32, 128), F32),
-            dma((6,)), dma,
+            pltpu.SemaphoreType.REGULAR, dma((6,)), dma,
             dma((2, 4)), dma((2,)), dma((2, 4)), dma((2,)), dma((2,)),
             dma((4,)), dma, dma((4,)), dma, dma,
             dma((3,)), dma((3,)), dma((2, 3)), dma((2, 3)),

time: 69.6 us -> 71.2 us (1.023)
  Pallas kernels: 68 us -> 69.6 us
    pallas_call x1, Pallas kernels: 68 us -> 69.6 us  [on_device(): pl.pallas_call(kernel, out_shape=pltpu.VMEM((1, 64, 2048), F32), in_specs...]
where the time goes in v6:
time: 71.2 us; the launch traced here: 71 us
  Pallas kernels  69.6 us (98%)
  local copies, waits for them, and re-layouts  0.8 us (1%)
    pallas_call x1, Pallas kernels, on_device(): pl.pallas_call(kernel, out_shape=pltpu.VMEM((1, 64, 2048), F32), in_specs...  69.6 us

profile of v6, /device:TPU:1, one launch (start us, length us, event | category | flops | bytes accessed | tf_op | source)
XLA Modules:
  0.0 71.0 jit_solution(3438335334876192890)
XLA Ops:
  0.7 69.6 %coarse_operator.1 = f32[1,64,2048]{2,1,0:T(8,128)S(1)} custom-call(bf16[1,1,16,320,320]{4,3,2,1,0:T(8,128)(2,1)} %a_hbm.1, s32[1,1,16]{2,1,0:T(1,128)} %rows_hbm.1, s32[1,1,16]{2,1,0:T(1,128)} %cols_hbm.1, s32[1,1]{1,0:T(1,128)S(6)} %copy.10.count_hbm, bf16[4,64,320]{2,1,0:T(8,128)(2,1)} %bitcast.1, s32[4]{0:T(128)} %agg_hbm.1, s32[32]{0:T(128)} %relay_hbm.1), custom_call_target="tpu_custom_call" | custom-call | tf_op jit(solution)/shard_map/coarse_operator/pallas_call | solution.py:405
  70.2 0.8 %copy.9 = f32[1,64,2048]{2,1,0:T(8,128)} copy(f32[1,64,2048]{2,1,0:T(8,128)S(1)} %coarse_operator.1) | data formatting | bytes 1048576

commit v7 on v5

--- a/solution.py
+++ b/solution.py
@@ -12,7 +12,7 @@
 NX, NY, NZ = 4, 4, 16
 TREE = (6, 10, 2, 14)
 FAR = (8, 6, 10, 4, 12, 2, 14)
-RING = (1, 15, 2, 14, 4, 12, 6, 10, 8)
+RING = (8, 6, 10, 4, 12, 2, 14, 1, 15)
 STEPS = 32767.0
 F32 = jnp.float32
 BF16 = jnp.bfloat16
@@ -121,14 +121,12 @@
         start_when(in_tree, [copy_to(1, 2), copy_to(15, 3)])
 
     quad_devs = (sib, quad_same, quad_diag)
-    quad_in = [start(remote(agg_mine, agg_quad.at[k + 1], q_ssem.at[k], q_rsem.at[k], quad_devs[k])) for k in range(3)]
     start_when(d == 0, [agg_copy(at_z(step), ag_ssem.at[k]) for k, step in enumerate(TREE)])
     p_out = [[p_copy(t, at_z(step), p_ssem.at[t, k]) for k, step in enumerate(TREE)] for t in range(2)]
 
-    @pl.when(d == 0)
-    def _():
-        for copy in p_out[0]:
-            copy.start()
+    for t in range(2):
+        start_when(d == 0, p_out[t])
+    quad_in = [start(remote(agg_mine, agg_quad.at[k + 1], q_ssem.at[k], q_rsem.at[k], quad_devs[k])) for k in range(3)]
 
     loads[5].wait()
 
@@ -140,16 +138,7 @@
         lhl[s, 0:64] = high
         lhl[s, 64:128] = (left - high.astype(F32)).astype(BF16)
 
-    pl.loop(0, 8)(left_product)
-
-    @pl.when(d == 0)
-    def _():
-        for copy in p_out[0]:
-            copy.wait_send()
-
-    start_when(d == 0, p_out[1])
-
-    pl.loop(8, 16)(left_product)
+    pl.loop(0, 16)(left_product)
 
     for copy in quad_in:
         copy.wait_recv()
@@ -168,7 +157,6 @@
         for g in range(16):
             at = jnp.where(labels[g] == wanted, g + 1, at)
         rows_s[1, k] = at
-
 
     @pl.when(d != 0)
     def _():

time: 69.6 us -> 69.2 us (level)
  no operation moved by 1% of the time
where the time goes in v7:
time: 69.2 us; the launch traced here: 69 us
  Pallas kernels  67.6 us (98%)
  local copies, waits for them, and re-layouts  0.8 us (1%)
    pallas_call x1, Pallas kernels, on_device(): pl.pallas_call(kernel, out_shape=pltpu.VMEM((1, 64, 2048), F32), in_specs...  67.6 us

profile of v7, /device:TPU:1, one launch (start us, length us, event | category | flops | bytes accessed | tf_op | source)
XLA Modules:
  0.0 69.0 jit_solution(5409242647793896303)
XLA Ops:
  0.7 67.6 %coarse_operator.1 = f32[1,64,2048]{2,1,0:T(8,128)S(1)} custom-call(bf16[1,1,16,320,320]{4,3,2,1,0:T(8,128)(2,1)} %a_hbm.1, s32[1,1,16]{2,1,0:T(1,128)} %rows_hbm.1, s32[1,1,16]{2,1,0:T(1,128)} %cols_hbm.1, s32[1,1]{1,0:T(1,128)S(6)} %copy.10.count_hbm, bf16[4,64,320]{2,1,0:T(8,128)(2,1)} %bitcast.1, s32[4]{0:T(128)} %agg_hbm.1, s32[32]{0:T(128)} %relay_hbm.1), custom_call_target="tpu_custom_call" | custom-call | tf_op jit(solution)/shard_map/coarse_operator/pallas_call | solution.py:387
  68.2 0.8 %copy.9 = f32[1,64,2048]{2,1,0:T(8,128)} copy(f32[1,64,2048]{2,1,0:T(8,128)S(1)} %coarse_operator.1) | data formatting | bytes 1048576
